TPU v7x, 512 devices: a whole 4x8x8 slice. The times are simulated.
512 devices in a mesh: seq: 64 (over z, x, core), tp: 8 (over y).
Axes of the slice: x: 4, y: 8, z: 8, core: 2. Of those that a mesh axis runs over, the one named last changes fastest.
Arguments:
- query_beam: bfloat16 [32768, 5120], P(('seq', 'tp')), may hold values from -6 to 6
- key_value_beam: bfloat16 [32768, 2048], P(('seq', 'tp')), may hold values from -24 to 24, as said below
- beam_row_index: int32 [32768], replicated, may hold values from 0 to 32767, as said below
- ancestors: int32 [256, 10], P('seq'), may hold values from 0 to 255, as said below
- depth: int32 [256], P('seq'), may hold values from 0 to 10, as said below
Outputs:
- attended: bfloat16 [32768, 5120], P('seq', 'tp')
Inputs may be any that keep to these rules, and one draw needn't show every extreme that they name: A permutation of the packed rows: beam_row_index[p] is the beam row that lands at packed row p. Each beam device, holding 64 rows, holds exactly 1 row of each packed shard of 512 rows. For j < depth[g], ancestors[g, j] is the block at depth j on the path from the root of g's tree to g, an earlier block; the slots from depth[g] on hold g itself. A tree is 32 consecutive blocks, and its first 3 blocks form a chain. `depth`: the number of ancestors of each block. `key_value_beam`: keys lie within -5 to 5.
All inputs are finite; a program needn't handle non-finite values.
Results may differ from a plain program's by a relative error of at most 0.0048.
Values may be sent and summed in bfloat16 or wider, within the bound.
No kernel may reach another device: no remote copies, remote signals or barrier semaphores. Data moves between devices by JAX's collectives and lax.ppermute only.
A program may use at most 64 MiB of HBM per device.

v0:
```python
import math

import jax
import jax.numpy as jnp
from jax import lax
from jax.sharding import PartitionSpec as P

HEAD_WIDTH = 128
BLOCK_TOKENS = 128
ANCESTOR_SLOTS = 10
TREE_SHARDS = 8


def shifted_2(block, axis, distance):
    devices = range(lax.axis_size(axis))
    route = [(i - distance, i) for i in devices if i - distance in devices]
    return lax.ppermute(block, axis, route)


def select_rows(target, source_rows):
    count = source_rows.shape[0]
    picker = (target[:, None] == jnp.arange(count, dtype=jnp.int32)[None, :]).astype(jnp.bfloat16)
    return jnp.dot(picker, source_rows, preferred_element_type=jnp.float32).astype(jnp.bfloat16)


def count_rank(values):
    return jnp.sum((values[None, :] < values[:, None]).astype(jnp.int32), 1)


def packed_slots(beam_row_index, my_shard, tok_dev, beam_dev, rows_peer, tiles):
    my_rows = lax.dynamic_slice_in_dim(beam_row_index, my_shard * tok_dev, tok_dev)
    source = my_rows // beam_dev
    within = jnp.arange(tok_dev, dtype=jnp.int32)
    ranked = count_rank(source * tok_dev + within)
    rank_in = ranked - source * rows_peer
    return (source // tiles * rows_peer + rank_in) * tiles + source % tiles


def dense_block(query_rows, distant_blocks, current, levels):
    inv_root = 1.0 / math.sqrt(HEAD_WIDTH)
    key_rows = jnp.concatenate(
        [distant_blocks.reshape((ANCESTOR_SLOTS * BLOCK_TOKENS,) + current.shape[1:]), current], 0
    )
    scores = (
        jnp.einsum(
            "bkgd,nkd->kgbn", query_rows, key_rows[:, :, 0], preferred_element_type=jnp.float32
        )
        * inv_root
    )
    slot_of = jnp.arange((ANCESTOR_SLOTS + 1) * BLOCK_TOKENS, dtype=jnp.int32) // BLOCK_TOKENS
    offset = (
        jnp.arange((ANCESTOR_SLOTS + 1) * BLOCK_TOKENS, dtype=jnp.int32)
        - ANCESTOR_SLOTS * BLOCK_TOKENS
    )
    query_pos = jnp.arange(BLOCK_TOKENS, dtype=jnp.int32)[:, None]
    allowed = jnp.where(
        slot_of[None] < ANCESTOR_SLOTS, slot_of[None] < levels, offset[None] <= query_pos
    )
    scores = jnp.where(allowed, scores, -jnp.inf)
    largest = jnp.max(scores, -1, keepdims=True)
    shifted = jnp.exp(scores - largest)
    normalizer = jnp.sum(shifted, -1, keepdims=True)
    weights = (shifted / normalizer).astype(jnp.bfloat16)
    return jnp.einsum(
        "kgbn,nkd->bkgd", weights, key_rows[:, :, 1], preferred_element_type=jnp.float32
    )


def body(query_beam, key_value_beam, beam_row_index, ancestors, depth):
    shards = lax.axis_size("seq")
    tiles = lax.axis_size("tp")
    beam_dev = query_beam.shape[0]
    tok_dev = beam_dev * tiles
    rows_peer = beam_dev // shards
    blk_dev = tok_dev // BLOCK_TOKENS
    everyone = beam_row_index.shape[0]
    my_shard = lax.axis_index("seq")
    device = my_shard * tiles + lax.axis_index("tp")
    local_ids = device * beam_dev + jnp.arange(beam_dev, dtype=jnp.int32)
    matched = beam_row_index[None, :] == local_ids[:, None]
    my_rows = jnp.sum(jnp.where(matched, jnp.arange(everyone, dtype=jnp.int32)[None, :], 0), 1)
    order_rank = count_rank(my_rows)
    sorter = (order_rank[None, :] == jnp.arange(beam_dev, dtype=jnp.int32)[:, None]).astype(
        jnp.bfloat16
    )
    query_sorted = jnp.dot(sorter, query_beam, preferred_element_type=jnp.float32).astype(
        jnp.bfloat16
    )
    pairs_sorted = jnp.dot(sorter, key_value_beam, preferred_element_type=jnp.float32).astype(
        jnp.bfloat16
    )
    query_out = query_sorted.reshape(shards, rows_peer, tiles, query_beam.shape[1] // tiles)
    pairs_out = pairs_sorted.reshape(shards, rows_peer, tiles, key_value_beam.shape[1] // tiles)
    query_in, pairs_in = (
        lax.all_to_all(
            lax.all_to_all(query_out, "seq", split_axis=0, concat_axis=0, tiled=True),
            "tp",
            split_axis=2,
            concat_axis=2,
            tiled=True,
        ),
        lax.all_to_all(
            lax.all_to_all(pairs_out, "seq", split_axis=0, concat_axis=0, tiled=True),
            "tp",
            split_axis=2,
            concat_axis=2,
            tiled=True,
        ),
    )
    placed = packed_slots(beam_row_index, my_shard, tok_dev, beam_dev, rows_peer, tiles)
    query_rows = select_rows(placed, query_in.reshape(tok_dev, -1))
    head_pairs = select_rows(placed, pairs_in.reshape(tok_dev, -1))
    earlier = [
        shifted_2(head_pairs, "seq", TREE_SHARDS - 1 - back_step)
        for back_step in range(TREE_SHARDS - 1)
    ]
    window = jnp.stack(earlier + [head_pairs], 0)
    kv_heads = head_pairs.shape[1] // (2 * HEAD_WIDTH)
    queries_per_group = query_rows.shape[1] // (kv_heads * HEAD_WIDTH)
    window_count = TREE_SHARDS * blk_dev
    window_flat = window.reshape(window_count, BLOCK_TOKENS * kv_heads * 2 * HEAD_WIDTH)
    first_block = (my_shard - TREE_SHARDS + 1) * blk_dev
    local_slot = jnp.clip(ancestors - first_block, 0, window_count - 1)
    slot_picker = (
        local_slot[:, :, None] == jnp.arange(window_count, dtype=jnp.int32)[None, None, :]
    ).astype(jnp.bfloat16)
    distant_all = jnp.einsum(
        "bsw,wx->bsx", slot_picker, window_flat, preferred_element_type=jnp.float32
    ).astype(jnp.bfloat16)
    distant_all = distant_all.reshape(
        blk_dev, ANCESTOR_SLOTS, BLOCK_TOKENS, kv_heads, 2, HEAD_WIDTH
    )
    query_blocks = query_rows.reshape(
        blk_dev, BLOCK_TOKENS, kv_heads, queries_per_group, HEAD_WIDTH
    )
    pair_blocks = head_pairs.reshape(blk_dev, BLOCK_TOKENS, kv_heads, 2, HEAD_WIDTH)

    def attend(packet):
        query_blk, current, distant_blocks, levels = packet
        result = dense_block(query_blk, distant_blocks, current, levels)
        return result.astype(jnp.bfloat16)

    attended = lax.map(attend, (query_blocks, pair_blocks, distant_all, depth))
    return attended.reshape(tok_dev, kv_heads * queries_per_group * HEAD_WIDTH)


def solution(mesh):
    return jax.shard_map(
        body,
        mesh=mesh,
        in_specs=(P(("seq", "tp"), None), P(("seq", "tp"), None), P(), P("seq", None), P("seq")),
        out_specs=P("seq", "tp"),
        check_vma=False,
    )
```

profile of v0, /device:TPU:64, one launch (start us, length us, event | category | flops | bytes accessed | tf_op | source)
XLA Modules:
  0.0 159.0 jit_solution(4369326307987796868)
XLA Ops:
  0.0 2.0 %select_reduce_fusion = s32[64]{0:T(128)S(1)} fusion(s32[32768]{0:T(1024)} %param.9, s32[64]{0:T(128)S(1)} %iota_add_fusion.2), kind=kLoop, calls=%fused_computation.38 | loop fusion | flops 6291392 | bytes 131584 | tf_op jit(solution)/shard_map/reduce_sum | solution.py:81
  2.2 1.2 convolution_convert_fusion.2
  3.4 0.8 copy.75
  4.1 13.0 %all-to-all-start = ((bf16[64,1,8,256]{3,2,1,0:T(8,128)(2,1)}), bf16[64,1,8,256]{3,2,1,0:T(8,128)(2,1)S(1)}, u32[]{:S(2)}, u32[]{:S(2)}) async-start(bf16[64,1,8,256]{3,2,1,0:T(8,128)(2,1)} %bitcast.14), calls=%async_computation | async-start | bytes 524288 | tf_op jit(solution)/shard_map/all_to_all | solution.py:103
  17.5 0.9 copy.76
  18.4 10.9 %all-to-all-done = bf16[64,1,8,256]{3,2,1,0:T(8,128)(2,1)S(1)} async-done(((bf16[64,1,8,256]{3,2,1,0:T(8,128)(2,1)}), bf16[64,1,8,256]{3,2,1,0:T(8,128)(2,1)S(1)}, u32[]{:S(2)}, u32[]{:S(2)}) %all-to-all-start) | async-done | bytes 262176 | tf_op jit(solution)/shard_map/all_to_all | solution.py:103
  29.3 0.8 copy.52
  30.0 7.1 %all-to-all-start.1 = ((bf16[64,1,8,256]{3,0,1,2:T(8,128)(2,1)}), bf16[64,1,8,256]{3,0,1,2:T(8,128)(2,1)S(1)}, u32[]{:S(2)}, u32[]{:S(2)}) async-start(bf16[64,1,8,256]{3,0,1,2:T(8,128)(2,1)} %copy.52), calls=%async_computation.1 | async-start | bytes 524288 | tf_op jit(solution)/shard_map/all_to_all | solution.py:102
  37.1 0.8 iota_add_fusion.1
  38.1 0.8 fusion.41
  38.9 10.8 %all-to-all-done.1 = bf16[64,1,8,256]{3,0,1,2:T(8,128)(2,1)S(1)} async-done(((bf16[64,1,8,256]{3,0,1,2:T(8,128)(2,1)}), bf16[64,1,8,256]{3,0,1,2:T(8,128)(2,1)S(1)}, u32[]{:S(2)}, u32[]{:S(2)}) %all-to-all-start.1) | async-done | bytes 262176 | tf_op jit(solution)/shard_map/all_to_all | solution.py:102
  49.7 5.2 %all-to-all-start.2 = ((bf16[64,1,8,640]{3,2,1,0:T(8,128)(2,1)}), bf16[64,1,8,640]{3,2,1,0:T(8,128)(2,1)S(1)}, u32[]{:S(2)}, u32[]{:S(2)}) async-start(bf16[64,1,8,640]{3,2,1,0:T(8,128)(2,1)} %bitcast.24), calls=%async_computation.2 | async-start | bytes 1310720 | tf_op jit(solution)/shard_map/all_to_all | solution.py:96
  55.3 4.3 %collective-permute-start = (bf16[512,256]{1,0:T(8,128)(2,1)S(1)}, bf16[512,256]{1,0:T(8,128)(2,1)S(1)}, u32[]{:S(2)}, u32[]{:S(2)}) collective-permute-start(bf16[512,256]{1,0:T(8,128)(2,1)S(1)} %convolution_convert_fusion.4), channel_id=1, source_target_pairs={{0,56},{8,64},{16,72},{24,80},{32,88},{40,96},{48,104},{56,112},{6... | collective-permute-start | bytes 786440 | tf_op jit(solution)/shard_map/ppermute | solution.py:17
  59.6 3.7 %collective-permute-start.1 = (bf16[512,256]{1,0:T(8,128)(2,1)S(1)}, bf16[512,256]{1,0:T(8,128)(2,1)S(1)}, u32[]{:S(2)}, u32[]{:S(2)}) collective-permute-start(bf16[512,256]{1,0:T(8,128)(2,1)S(1)} %convolution_convert_fusion.4), channel_id=1, source_target_pairs={{0,48},{8,56},{16,64},{24,72},{32,80},{40,88},{48,96},{56,104},{64... | collective-permute-start | bytes 786440 | tf_op jit(solution)/shard_map/ppermute | solution.py:17
  63.4 3.1 %collective-permute-start.2 = (bf16[512,256]{1,0:T(8,128)(2,1)S(1)}, bf16[512,256]{1,0:T(8,128)(2,1)S(1)}, u32[]{:S(2)}, u32[]{:S(2)}) collective-permute-start(bf16[512,256]{1,0:T(8,128)(2,1)S(1)} %convolution_convert_fusion.4), channel_id=1, source_target_pairs={{0,40},{8,48},{16,56},{24,64},{32,72},{40,80},{48,88},{56,96},{64,... | collective-permute-start | bytes 786440 | tf_op jit(solution)/shard_map/ppermute | solution.py:17
  66.5 4.6 %collective-permute-start.3 = (bf16[512,256]{1,0:T(8,128)(2,1)S(1)}, bf16[512,256]{1,0:T(8,128)(2,1)S(1)}, u32[]{:S(2)}, u32[]{:S(2)}) collective-permute-start(bf16[512,256]{1,0:T(8,128)(2,1)S(1)} %convolution_convert_fusion.4), channel_id=1, source_target_pairs={{0,32},{8,40},{16,48},{24,56},{32,64},{40,72},{48,80},{56,88},{64,... | collective-permute-start | bytes 786440 | tf_op jit(solution)/shard_map/ppermute | solution.py:17
  71.1 2.5 %collective-permute-start.4 = (bf16[512,256]{1,0:T(8,128)(2,1)S(1)}, bf16[512,256]{1,0:T(8,128)(2,1)S(1)}, u32[]{:S(2)}, u32[]{:S(2)}) collective-permute-start(bf16[512,256]{1,0:T(8,128)(2,1)S(1)} %convolution_convert_fusion.4), channel_id=1, source_target_pairs={{0,24},{8,32},{16,40},{24,48},{32,56},{40,64},{48,72},{56,80},{64,... | collective-permute-start | bytes 786440 | tf_op jit(solution)/shard_map/ppermute | solution.py:17
  73.7 5.1 %collective-permute-start.5 = (bf16[512,256]{1,0:T(8,128)(2,1)S(1)}, bf16[512,256]{1,0:T(8,128)(2,1)S(1)}, u32[]{:S(2)}, u32[]{:S(2)}) collective-permute-start(bf16[512,256]{1,0:T(8,128)(2,1)S(1)} %convolution_convert_fusion.4), channel_id=1, source_target_pairs={{0,16},{8,24},{16,32},{24,40},{32,48},{40,56},{48,64},{56,72},{64,... | collective-permute-start | bytes 786440 | tf_op jit(solution)/shard_map/ppermute | solution.py:17
  79.5 3.4 %collective-permute-done.1 = bf16[512,256]{1,0:T(8,128)(2,1)S(1)} collective-permute-done((bf16[512,256]{1,0:T(8,128)(2,1)S(1)}, bf16[512,256]{1,0:T(8,128)(2,1)S(1)}, u32[]{:S(2)}, u32[]{:S(2)}) %collective-permute-start.1) | collective-permute-done | bytes 262176 | tf_op jit(solution)/shard_map/ppermute | solution.py:17
  82.9 1.9 %collective-permute-start.6 = (bf16[512,256]{1,0:T(8,128)(2,1)S(1)}, bf16[512,256]{1,0:T(8,128)(2,1)S(1)}, u32[]{:S(2)}, u32[]{:S(2)}) collective-permute-start(bf16[512,256]{1,0:T(8,128)(2,1)S(1)} %convolution_convert_fusion.4), channel_id=1, source_target_pairs={{0,8},{8,16},{16,24},{24,32},{32,40},{40,48},{48,56},{56,64},{64,7... | collective-permute-start | bytes 786440 | tf_op jit(solution)/shard_map/ppermute | solution.py:17
  86.3 9.7 %collective-permute-done.3 = bf16[512,256]{1,0:T(8,128)(2,1)S(1)} collective-permute-done((bf16[512,256]{1,0:T(8,128)(2,1)S(1)}, bf16[512,256]{1,0:T(8,128)(2,1)S(1)}, u32[]{:S(2)}, u32[]{:S(2)}) %collective-permute-start.3) | collective-permute-done | bytes 262176 | tf_op jit(solution)/shard_map/ppermute | solution.py:17
  96.6 0.9 copy.56
  97.6 4.4 %all-to-all-start.3 = ((bf16[64,1,8,640]{3,0,1,2:T(8,128)(2,1)}), bf16[64,1,8,640]{3,0,1,2:T(8,128)(2,1)}, u32[]{:S(2)}, u32[]{:S(2)}) async-start(bf16[64,1,8,640]{3,0,1,2:T(8,128)(2,1)} %copy.56), calls=%async_computation.3 | async-start | bytes 1310720 | tf_op jit(solution)/shard_map/all_to_all | solution.py:95
  102.0 0.7 bitcast_dynamic-update-slice_fusion.3
  102.7 4.3 %collective-permute-done.5 = bf16[512,256]{1,0:T(8,128)(2,1)S(1)} collective-permute-done((bf16[512,256]{1,0:T(8,128)(2,1)S(1)}, bf16[512,256]{1,0:T(8,128)(2,1)S(1)}, u32[]{:S(2)}, u32[]{:S(2)}) %collective-permute-start.5) | collective-permute-done | bytes 262176 | tf_op jit(solution)/shard_map/ppermute | solution.py:17
  107.7 1.6 %collective-permute-done.6 = bf16[512,256]{1,0:T(8,128)(2,1)S(1)} collective-permute-done((bf16[512,256]{1,0:T(8,128)(2,1)S(1)}, bf16[512,256]{1,0:T(8,128)(2,1)S(1)}, u32[]{:S(2)}, u32[]{:S(2)}) %collective-permute-start.6) | collective-permute-done | bytes 262176 | tf_op jit(solution)/shard_map/ppermute | solution.py:17
  110.0 0.7 bitcast_dynamic-update-slice_fusion
  110.7 2.9 %reshape.128 = bf16[32,32768,1]{1,0,2:T(8,128)(2,1)S(1)} reshape(bf16[8,512,256]{2,1,0:T(8,128)(2,1)} %bitcast_dynamic-update-slice_fusion) | data formatting | bytes 4194304 | tf_op jit(solution)/shard_map/reshape | solution.py:121
  113.6 3.2 %convolution_convert_fusion = bf16[4,10,32768]{2,1,0:T(8,128)(2,1)} fusion(bf16[32,32768,1]{1,0,2:T(8,128)(2,1)S(1)} %reshape.128, s32[4,10]{1,0:T(4,128)S(1)} %subtract_clamp_fusion), kind=kOutput, calls=%fused_computation.37 | convolution fusion | flops 85198080 | bytes 4718752 | tf_op jit(solution)/shard_map/bsw,wx->bsx/dot_general | solution.py:127
  116.9 3.9 %reshape.130 = bf16[4,10,128,1,2,128]{5,4,2,1,0,3:T(2,128)(2,1)S(1)} reshape(bf16[4,10,32768]{2,1,0:T(8,128)(2,1)} %convolution_convert_fusion) | data formatting | bytes 5242880 | tf_op jit(solution)/shard_map/reshape | solution.py:130
  121.0 2.8 %convolution_convert_fusion.3 = bf16[512,640]{1,0:T(8,128)(2,1)} fusion(bf16[64,1,8,640]{3,0,1,2:T(8,128)(2,1)} %all-to-all-done.3, s32[512]{0:T(512)S(1)} %fusion.41), kind=kOutput, calls=%fused_computation.41 | convolution fusion | flops 336134144 | bytes 1312768 | tf_op jit(solution)/shard_map/dot_general | solution.py:23
  123.7 2.5 %reshape.131 = bf16[4,128,1,5,128]{4,3,1,0,2:T(8,128)(2,1)} reshape(bf16[512,640]{1,0:T(8,128)(2,1)} %convolution_convert_fusion.3) | data formatting | bytes 1310720 | tf_op jit(solution)/shard_map/reshape | solution.py:133
  126.3 2.3 %copy.61 = bf16[4,128,1,5,128]{4,1,3,2,0:T(8,128)(2,1)} copy(bf16[4,128,1,5,128]{4,3,1,0,2:T(8,128)(2,1)} %reshape.131) | data formatting | bytes 1310720 | tf_op jit(solution)/shard_map/while | solution.py:143
  128.5 27.9 %while.12 = (s32[]{:T(128)}, bf16[4,128,1,5,128]{1,4,3,2,0:T(8,128)(2,1)}, bf16[4,10,128,1,2,128]{5,4,2,1,0,3:T(2,128)(2,1)S(1)}, bf16[4,128,1,2,128]{4,3,1,0,2:...) while((s32[]{:T(128)}, bf16[4,128,1,5,128]{1,4,3,2,0:T(8,128)(2,1)}, ...), condition=%wide.region_6.7_spmd, body=%wide.region_3.6_spmd.sunk | while | flops 470480768 | bytes 15857765 | solution.py:143
  129.9 1.2 fusion.59
  131.9 1.6 %fusion.60 = (f32[5,128]{1,0:T(8,128)S(1)}, f32[1,5,128,1408]{2,3,1,0:T(8,128)S(1)}) fusion(bf16[4,128,1,5,128]{4,1,3,2,0:T(8,128)(2,1)} %get-tuple-element.195, s32[]{:T(128)} %get-tuple-element.183, bf16[128,1,2,128]{3,0,2,1:T(8,128)(2,1)S(1)} %bitcast.104, bf16[1280,1,2,128]{3,0,2,1:T(8,128)(2,1)S(1)} %bitcast.102, pred[128,1408]{0,1:T(8,128)(4,1)S(1)} %fusion.59), kind=kOutput, calls=%fused_computation.87.clone.1 | convolution fusion | flops 234110336 | bytes 4672512 | tf_op jit(solution)/shard_map/while/body/eval_jaxpr/bkgd,nkd->kgbn/dot_general | solution.py:45
  134.0 1.5 fusion.62
  136.9 1.2 fusion.59
  138.9 1.6 %fusion.60 = (f32[5,128]{1,0:T(8,128)S(1)}, f32[1,5,128,1408]{2,3,1,0:T(8,128)S(1)}) fusion(bf16[4,128,1,5,128]{4,1,3,2,0:T(8,128)(2,1)} %get-tuple-element.195, s32[]{:T(128)} %get-tuple-element.183, bf16[128,1,2,128]{3,0,2,1:T(8,128)(2,1)S(1)} %bitcast.104, bf16[1280,1,2,128]{3,0,2,1:T(8,128)(2,1)S(1)} %bitcast.102, pred[128,1408]{0,1:T(8,128)(4,1)S(1)} %fusion.59), kind=kOutput, calls=%fused_computation.87.clone.1 | convolution fusion | flops 234110336 | bytes 4672512 | tf_op jit(solution)/shard_map/while/body/eval_jaxpr/bkgd,nkd->kgbn/dot_general | solution.py:45
  141.0 1.5 fusion.62
  143.9 1.2 fusion.59
  145.8 1.6 %fusion.60 = (f32[5,128]{1,0:T(8,128)S(1)}, f32[1,5,128,1408]{2,3,1,0:T(8,128)S(1)}) fusion(bf16[4,128,1,5,128]{4,1,3,2,0:T(8,128)(2,1)} %get-tuple-element.195, s32[]{:T(128)} %get-tuple-element.183, bf16[128,1,2,128]{3,0,2,1:T(8,128)(2,1)S(1)} %bitcast.104, bf16[1280,1,2,128]{3,0,2,1:T(8,128)(2,1)S(1)} %bitcast.102, pred[128,1408]{0,1:T(8,128)(4,1)S(1)} %fusion.59), kind=kOutput, calls=%fused_computation.87.clone.1 | convolution fusion | flops 234110336 | bytes 4672512 | tf_op jit(solution)/shard_map/while/body/eval_jaxpr/bkgd,nkd->kgbn/dot_general | solution.py:45
  147.9 1.5 fusion.62
  150.8 1.2 fusion.59
  152.8 1.6 %fusion.60 = (f32[5,128]{1,0:T(8,128)S(1)}, f32[1,5,128,1408]{2,3,1,0:T(8,128)S(1)}) fusion(bf16[4,128,1,5,128]{4,1,3,2,0:T(8,128)(2,1)} %get-tuple-element.195, s32[]{:T(128)} %get-tuple-element.183, bf16[128,1,2,128]{3,0,2,1:T(8,128)(2,1)S(1)} %bitcast.104, bf16[1280,1,2,128]{3,0,2,1:T(8,128)(2,1)S(1)} %bitcast.102, pred[128,1408]{0,1:T(8,128)(4,1)S(1)} %fusion.59), kind=kOutput, calls=%fused_computation.87.clone.1 | convolution fusion | flops 234110336 | bytes 4672512 | tf_op jit(solution)/shard_map/while/body/eval_jaxpr/bkgd,nkd->kgbn/dot_general | solution.py:45
  154.9 1.5 fusion.62
  156.4 1.6 %copy.71 = bf16[4,128,1,5,128]{4,3,1,0,2:T(8,128)(2,1)S(1)} copy(bf16[4,128,1,5,128]{1,4,3,2,0:T(8,128)(2,1)} %get-tuple-element.84) | data formatting | bytes 1310720 | tf_op jit(solution)/shard_map/reshape | solution.py:144
  158.0 0.9 copy.89
  (57 shorter events, 16.0 us)
Async XLA Ops:
  0.0 17.1 %copy-start = (bf16[64,5120]{1,0:T(8,128)(2,1)S(1)}, bf16[64,5120]{1,0:T(8,128)(2,1)}, u32[]{:S(2)}) copy-start(bf16[64,5120]{1,0:T(8,128)(2,1)} %param.7) | copy-start | bytes 1966084
  4.1 25.2 %all-to-all-start = ((bf16[64,1,8,256]{3,2,1,0:T(8,128)(2,1)}), bf16[64,1,8,256]{3,2,1,0:T(8,128)(2,1)S(1)}, u32[]{:S(2)}, u32[]{:S(2)}) async-start(bf16[64,1,8,256]{3,2,1,0:T(8,128)(2,1)} %bitcast.14), calls=%async_computation | async-start | bytes 524288 | tf_op jit(solution)/shard_map/all_to_all | solution.py:103
  17.4 45.9 %copy-start.1 = (s32[4,10]{1,0:T(4,128)S(1)}, s32[4,10]{1,0:T(4,128)}, u32[]{:S(2)}) copy-start(s32[4,10]{1,0:T(4,128)} %param.10) | copy-start | bytes 484
  30.0 19.7 %all-to-all-start.1 = ((bf16[64,1,8,256]{3,0,1,2:T(8,128)(2,1)}), bf16[64,1,8,256]{3,0,1,2:T(8,128)(2,1)S(1)}, u32[]{:S(2)}, u32[]{:S(2)}) async-start(bf16[64,1,8,256]{3,0,1,2:T(8,128)(2,1)} %copy.52), calls=%async_computation.1 | async-start | bytes 524288 | tf_op jit(solution)/shard_map/all_to_all | solution.py:102
  49.7 47.0 %all-to-all-start.2 = ((bf16[64,1,8,640]{3,2,1,0:T(8,128)(2,1)}), bf16[64,1,8,640]{3,2,1,0:T(8,128)(2,1)S(1)}, u32[]{:S(2)}, u32[]{:S(2)}) async-start(bf16[64,1,8,640]{3,2,1,0:T(8,128)(2,1)} %bitcast.24), calls=%async_computation.2 | async-start | bytes 1310720 | tf_op jit(solution)/shard_map/all_to_all | solution.py:96
  55.3 18.4 %collective-permute-start = (bf16[512,256]{1,0:T(8,128)(2,1)S(1)}, bf16[512,256]{1,0:T(8,128)(2,1)S(1)}, u32[]{:S(2)}, u32[]{:S(2)}) collective-permute-start(bf16[512,256]{1,0:T(8,128)(2,1)S(1)} %convolution_convert_fusion.4), channel_id=1, source_target_pairs={{0,56},{8,64},{16,72},{24,80},{32,88},{40,96},{48,104},{56,112},{6... | collective-permute-start | bytes 786440 | tf_op jit(solution)/shard_map/ppermute | solution.py:17
  59.6 23.3 %collective-permute-start.1 = (bf16[512,256]{1,0:T(8,128)(2,1)S(1)}, bf16[512,256]{1,0:T(8,128)(2,1)S(1)}, u32[]{:S(2)}, u32[]{:S(2)}) collective-permute-start(bf16[512,256]{1,0:T(8,128)(2,1)S(1)} %convolution_convert_fusion.4), channel_id=1, source_target_pairs={{0,48},{8,56},{16,64},{24,72},{32,80},{40,88},{48,96},{56,104},{64... | collective-permute-start | bytes 786440 | tf_op jit(solution)/shard_map/ppermute | solution.py:17
  63.4 22.2 %collective-permute-start.2 = (bf16[512,256]{1,0:T(8,128)(2,1)S(1)}, bf16[512,256]{1,0:T(8,128)(2,1)S(1)}, u32[]{:S(2)}, u32[]{:S(2)}) collective-permute-start(bf16[512,256]{1,0:T(8,128)(2,1)S(1)} %convolution_convert_fusion.4), channel_id=1, source_target_pairs={{0,40},{8,48},{16,56},{24,64},{32,72},{40,80},{48,88},{56,96},{64,... | collective-permute-start | bytes 786440 | tf_op jit(solution)/shard_map/ppermute | solution.py:17
  66.5 29.5 %collective-permute-start.3 = (bf16[512,256]{1,0:T(8,128)(2,1)S(1)}, bf16[512,256]{1,0:T(8,128)(2,1)S(1)}, u32[]{:S(2)}, u32[]{:S(2)}) collective-permute-start(bf16[512,256]{1,0:T(8,128)(2,1)S(1)} %convolution_convert_fusion.4), channel_id=1, source_target_pairs={{0,32},{8,40},{16,48},{24,56},{32,64},{40,72},{48,80},{56,88},{64,... | collective-permute-start | bytes 786440 | tf_op jit(solution)/shard_map/ppermute | solution.py:17
  71.1 30.9 %collective-permute-start.4 = (bf16[512,256]{1,0:T(8,128)(2,1)S(1)}, bf16[512,256]{1,0:T(8,128)(2,1)S(1)}, u32[]{:S(2)}, u32[]{:S(2)}) collective-permute-start(bf16[512,256]{1,0:T(8,128)(2,1)S(1)} %convolution_convert_fusion.4), channel_id=1, source_target_pairs={{0,24},{8,32},{16,40},{24,48},{32,56},{40,64},{48,72},{56,80},{64,... | collective-permute-start | bytes 786440 | tf_op jit(solution)/shard_map/ppermute | solution.py:17
  73.7 33.3 %collective-permute-start.5 = (bf16[512,256]{1,0:T(8,128)(2,1)S(1)}, bf16[512,256]{1,0:T(8,128)(2,1)S(1)}, u32[]{:S(2)}, u32[]{:S(2)}) collective-permute-start(bf16[512,256]{1,0:T(8,128)(2,1)S(1)} %convolution_convert_fusion.4), channel_id=1, source_target_pairs={{0,16},{8,24},{16,32},{24,40},{32,48},{40,56},{48,64},{56,72},{64,... | collective-permute-start | bytes 786440 | tf_op jit(solution)/shard_map/ppermute | solution.py:17
  82.9 26.4 %collective-permute-start.6 = (bf16[512,256]{1,0:T(8,128)(2,1)S(1)}, bf16[512,256]{1,0:T(8,128)(2,1)S(1)}, u32[]{:S(2)}, u32[]{:S(2)}) collective-permute-start(bf16[512,256]{1,0:T(8,128)(2,1)S(1)} %convolution_convert_fusion.4), channel_id=1, source_target_pairs={{0,8},{8,16},{16,24},{24,32},{32,40},{40,48},{48,56},{56,64},{64,7... | collective-permute-start | bytes 786440 | tf_op jit(solution)/shard_map/ppermute | solution.py:17
  97.6 23.4 %all-to-all-start.3 = ((bf16[64,1,8,640]{3,0,1,2:T(8,128)(2,1)}), bf16[64,1,8,640]{3,0,1,2:T(8,128)(2,1)}, u32[]{:S(2)}, u32[]{:S(2)}) async-start(bf16[64,1,8,640]{3,0,1,2:T(8,128)(2,1)} %copy.56), calls=%async_computation.3 | async-start | bytes 1310720 | tf_op jit(solution)/shard_map/all_to_all | solution.py:95
  123.7 4.8 %copy-start.2 = (s32[4]{0:T(128)S(1)}, s32[4]{0:T(128)}, u32[]{:S(2)}) copy-start(s32[4]{0:T(128)} %param.11) | copy-start | bytes 52
where the time goes:
time: 160 us; the launch traced here: 159 us
  starting transfers between devices  54.9 us (34%)
  waiting for transfers between devices  40.8 us (25%)
  local copies, waits for them, and re-layouts  28.9 us (18%)
  matrix products  20.3 us (13%)
  other arithmetic  13.6 us (8%)
    ppermute x7, starting transfers between devices, shifted_2(): return lax.ppermute(block, axis, route)  25.3 us
    ppermute x7, waiting for transfers between devices, shifted_2(): return lax.ppermute(block, axis, route)  19 us
    all_to_all x1, starting transfers between devices, body(): lax.all_to_all(pairs_out, 'seq', split_axis=0, concat_axis=0, tiled=True)  13 us
    all_to_all x1, waiting for transfers between devices, body(): lax.all_to_all(pairs_out, 'seq', split_axis=0, concat_axis=0, tiled=True)  10.9 us
    all_to_all x1, waiting for transfers between devices, body(): lax.all_to_all(lax.all_to_all(pairs_out, 'seq', split_axis=0, concat_axis...  10.8 us
    unnamed x16, local copies, waits for them, and re-layouts  7.67 us
    all_to_all x1, starting transfers between devices, body(): lax.all_to_all(lax.all_to_all(pairs_out, 'seq', split_axis=0, concat_axis...  7.1 us
    dot_general x4, matrix products, dense_block(): jnp.einsum('bkgd,nkd->kgbn', query_rows, key_rows[:, :, 0], preferred_ele...  6.38 us
  transfers between devices with their start and end apart: 11, of which 7 were waited for; matrix products, arithmetic and copies ran while one was open for 13% of the time, Pallas kernels for 0%

commit v1 on v0

v1 whole, which is shorter than its diff:
```python
import functools
import math

import jax
import jax.numpy as jnp
from jax import lax
from jax.experimental import pallas as pl
from jax.experimental.pallas import tpu as pltpu
from jax.sharding import Mesh
from jax.sharding import PartitionSpec as P

HEAD = 128
BLOCK = 128
SLOTS = 10
GROUP = 5
KEYS = (SLOTS + 1) * BLOCK
NEG = -1e30
VMEM_LIMIT = 40 * 1024 * 1024
NT = (((1,), (1,)), ((), ()))


def prep_kernel(place, index, query, pairs, out):
    device = place[0]
    idx = index[...]
    mine = (idx >> 6) == device
    local = jnp.where(mine, (idx & 63).astype(jnp.float32), 0.0).astype(jnp.bfloat16)
    shard = lax.broadcasted_iota(jnp.int32, (64, 256), 0)
    row = lax.broadcasted_iota(jnp.int32, (64, 256), 1)
    group = jnp.where((row >> 2) == shard, 1.0, 0.0).astype(jnp.bfloat16)
    by_shard = jnp.dot(group, local, preferred_element_type=jnp.float32)
    source = jnp.sum(by_shard, 1, keepdims=True).astype(jnp.int32)
    lane = lax.broadcasted_iota(jnp.int32, (64, 64), 1)
    picker = jnp.where(source == lane, 1.0, 0.0).astype(jnp.bfloat16)
    for t in range(8):
        q = jnp.dot(picker, query[:, t * 640 : (t + 1) * 640], preferred_element_type=jnp.float32)
        kv = jnp.dot(picker, pairs[:, t * 256 : (t + 1) * 256], preferred_element_type=jnp.float32)
        for z in range(8):
            out[z * 8 + t, :, :640] = q[z * 8 : (z + 1) * 8].astype(jnp.bfloat16)
            out[z * 8 + t, :, 640:] = kv[z * 8 : (z + 1) * 8].astype(jnp.bfloat16)


def arrival(idx, x, c, own):
    source = idx >> 6
    tail = ((source >> 6) << 3) | (source & 7)
    src_x, src_c = (source >> 4) & 3, (source >> 3) & 1
    if own:
        return (((src_x << 1) | src_c) << 6) | tail
    return ((((src_c ^ c) << 2) | ((x - src_x) & 3)) << 6) | tail


def picker_of(pos_row):
    column = jnp.transpose(jnp.broadcast_to(pos_row.astype(jnp.float32), (128, 128)))
    parts = []
    for k in range(4):
        lane = (lax.broadcasted_iota(jnp.int32, (128, 128), 1) + k * 128).astype(jnp.float32)
        parts.append(jnp.where(column == lane, 1.0, 0.0).astype(jnp.bfloat16))
    return jnp.concatenate(parts, 1)


def attend_kernel(
    place, ancestors, depth, index, query, a0, a1, a2, a3, b0, b1, b2, b3, out,
    keys, values, local_q, kc, vc, scores, probs,
):
    z, x, c = place[1], place[2], place[3]
    in_tree = x * 2 + c
    slabs = (a0, a1, a2, a3, b0, b1, b2, b3)

    def place_shard(j, carry):
        raw = jnp.concatenate([s[j] for s in slabs], 0)
        for n in range(4):
            idx = index[pl.ds(z * 32 + j * 4 + n, 1), :]
            pick = picker_of(arrival(idx, x, c, False))
            got = jnp.dot(pick, raw, preferred_element_type=jnp.float32).astype(jnp.bfloat16)
            keys[j * 4 + n] = got[:, :128]
            values[j * 4 + n] = got[:, 128:]
        return carry

    lax.fori_loop(0, in_tree + 1, place_shard, 0)
    for n in range(4):
        idx = index[pl.ds(z * 32 + in_tree * 4 + n, 1), :]
        pick = picker_of(arrival(idx, x, c, True))
        got = jnp.dot(pick, query[...], preferred_element_type=jnp.float32).astype(jnp.bfloat16)
        for h in range(GROUP):
            local_q[n, h * 128 : (h + 1) * 128, :] = got[:, h * 128 : (h + 1) * 128]
    vc[:, 128:] = jnp.ones((KEYS, 128), jnp.bfloat16)
    factor = math.log2(math.e) / math.sqrt(HEAD)

    def attend(b, carry):
        levels = depth[b]
        for j in range(SLOTS):
            block = ancestors[b, j] - z * 32
            kc[j * 128 : (j + 1) * 128, :] = keys[block]
            vc[j * 128 : (j + 1) * 128, :128] = values[block]
        me = in_tree * 4 + b
        kc[SLOTS * 128 :, :] = keys[me]
        vc[SLOTS * 128 :, :128] = values[me]
        scores[...] = lax.dot_general(local_q[b], kc[...], NT, preferred_element_type=jnp.float32)
        slot = lax.broadcasted_iota(jnp.int32, (1, SLOTS * 128), 1) >> 7
        bias = jnp.where(slot < levels, 0.0, NEG)
        r = lax.broadcasted_iota(jnp.int32, (128, 128), 0)
        n = lax.broadcasted_iota(jnp.int32, (128, 128), 1)
        causal = jnp.where(n <= r, 0.0, NEG)
        for h in range(GROUP):
            rows = slice(h * 128, (h + 1) * 128)
            s0 = scores[rows, : SLOTS * 128] + bias
            s1 = scores[rows, SLOTS * 128 :] + causal
            top = jnp.maximum(jnp.max(s0, 1, keepdims=True), jnp.max(s1, 1, keepdims=True))
            probs[rows, : SLOTS * 128] = jnp.exp2((s0 - top) * factor).astype(jnp.bfloat16)
            probs[rows, SLOTS * 128 :] = jnp.exp2((s1 - top) * factor).astype(jnp.bfloat16)
        acc = jnp.dot(probs[...], vc[...], preferred_element_type=jnp.float32)
        res = (acc[:, :128] / acc[:, 128:]).astype(jnp.bfloat16)
        for h in range(GROUP):
            out[pl.ds(pl.multiple_of(b * 128, 128), 128), h * 128 : (h + 1) * 128] = res[h * 128 : (h + 1) * 128]
        return carry

    lax.fori_loop(0, 4, attend, 0)


SMEM = pl.BlockSpec(memory_space=pltpu.SMEM)
VMEM = pl.BlockSpec(memory_space=pltpu.VMEM)


def shift(block, axis, size, distance):
    return lax.ppermute(block, axis, [(i, (i + distance) % size) for i in range(size)])


def body(query_beam, key_value_beam, beam_row_index, ancestors, depth):
    z, x, c, t = (lax.axis_index(n) for n in ("z", "x", "c", "t"))
    device = ((z * 4 + x) * 2 + c) * 8 + t
    place = jnp.stack([device, z, x, c]).astype(jnp.int32)
    index = beam_row_index.reshape(256, 128)
    packed = pl.pallas_call(
        prep_kernel,
        out_shape=jax.ShapeDtypeStruct((64, 8, 896), jnp.bfloat16),
        in_specs=[SMEM, VMEM, VMEM, VMEM],
        out_specs=VMEM,
        compiler_params=pltpu.CompilerParams(vmem_limit_bytes=VMEM_LIMIT),
        name="sort_rows",
    )(place, index, query_beam, key_value_beam)
    landed = lax.all_to_all(packed, ("z", "t"), split_axis=0, concat_axis=0, tiled=True)
    own = landed[:, :, 640:].transpose(1, 0, 2)
    query_out = landed[:, :, :640].transpose(1, 0, 2)
    same = [own] + [shift(own, "x", 4, d) for d in (1, 2, 3)]
    other = [shift(s, "c", 2, 1) for s in same]
    query = lax.all_to_all(query_out, ("x", "c"), split_axis=0, concat_axis=0, tiled=True)
    return pl.pallas_call(
        attend_kernel,
        out_shape=jax.ShapeDtypeStruct((512, 640), jnp.bfloat16),
        in_specs=[SMEM] * 3 + [VMEM] * 10,
        out_specs=VMEM,
        scratch_shapes=[
            pltpu.VMEM((32, 128, 128), jnp.bfloat16),
            pltpu.VMEM((32, 128, 128), jnp.bfloat16),
            pltpu.VMEM((4, 640, 128), jnp.bfloat16),
            pltpu.VMEM((KEYS, 128), jnp.bfloat16),
            pltpu.VMEM((KEYS, 256), jnp.bfloat16),
            pltpu.VMEM((640, KEYS), jnp.float32),
            pltpu.VMEM((640, KEYS), jnp.bfloat16),
        ],
        compiler_params=pltpu.CompilerParams(vmem_limit_bytes=VMEM_LIMIT),
        name="tree_attention",
    )(place, ancestors, depth, index, query.reshape(512, 640), *same, *other)


def solution(mesh):
    fine = Mesh(mesh.devices.reshape(8, 4, 2, 8), ("z", "x", "c", "t"))
    every, shard = ("z", "x", "c", "t"), ("z", "x", "c")
    return jax.shard_map(
        body,
        mesh=fine,
        in_specs=(P(every, None), P(every, None), P(), P(shard, None), P(shard)),
        out_specs=P(shard, "t"),
        check_vma=False,
    )
```

time: 160 us -> 95.2 us (0.59)
  the two profiles are of different devices: /device:TPU:64 before, /device:TPU:7 now
where the time goes in v1:
time: 95.2 us; the launch traced here: 94.7 us
  blocking collectives  41.1 us (43%)
  starting transfers between devices  27.2 us (29%)
  Pallas kernels  15.5 us (16%)
  waiting for transfers between devices  6.67 us (7%)
  local copies, waits for them, and re-layouts  4 us (4%)
    all_to_all x1, blocking collectives, body(): lax.all_to_all(packed, ('z', 't'), split_axis=0, concat_axis=0, tiled=True)  41.1 us
    ppermute x7, starting transfers between devices, shift(): lax.ppermute(block, axis, [(i, (i + distance) % size) for i in range(size)])  19.8 us
    pallas_call x1, Pallas kernels, body(): pl.pallas_call(attend_kernel, out_shape=jax.ShapeDtypeStruct((512, 640),...  14.4 us
    all_to_all x1, starting transfers between devices, body(): lax.all_to_all(query_out, ('x', 'c'), split_axis=0, concat_axis=0, tiled=...  7.38 us
    ppermute x7, waiting for transfers between devices, shift(): lax.ppermute(block, axis, [(i, (i + distance) % size) for i in range(size)])  6.67 us
    unnamed x13, local copies, waits for them, and re-layouts  3.01 us
  transfers between devices with their start and end apart: 8, of which 3 were waited for; matrix products, arithmetic and copies ran while one was open for 0% of the time, Pallas kernels for 0%

profile of v1, /device:TPU:7, one launch (start us, length us, event | category | flops | bytes accessed | tf_op | source)
XLA Modules:
  0.0 94.7 jit_solution(10049283563554581)
XLA Ops:
  0.0 0.1 pad_add_fusion.place
  0.1 0.0 copy-start
  0.1 1.1 %copy-done = bf16[64,5120]{1,0:T(8,128)(2,1)S(1)} copy-done((bf16[64,5120]{1,0:T(8,128)(2,1)S(1)}, bf16[64,5120]{1,0:T(8,128)(2,1)}, u32[]{:S(2)}) %copy-start) | copy-done | bytes 655384
  1.2 0.0 copy-start.1
  1.2 0.9 copy-done.1
  2.1 0.0 copy-start.3
  2.1 0.9 %copy-done.3 = bf16[64,2048]{1,0:T(8,128)(2,1)S(1)} copy-done((bf16[64,2048]{1,0:T(8,128)(2,1)S(1)}, bf16[64,2048]{1,0:T(8,128)(2,1)}, u32[]{:S(2)}) %copy-start.3) | copy-done | bytes 262168
  3.0 1.1 %sort_rows.1 = bf16[64,8,896]{2,1,0:T(8,128)(2,1)S(1)} custom-call(s32[4]{0:T(128)S(1)} %pad_add_fusion.place, s32[256,128]{1,0:T(8,128)S(1)} %bitcast.17, bf16[64,5120]{1,0:T(8,128)(2,1)S(1)} %copy-done, bf16[64,2048]{1,0:T(8,128)(2,1)S(1)} %copy-done.3), custom_call_target="tpu_custom_call" | custom-call | tf_op jit(solution)/shard_map/sort_rows/pallas_call | solution.py:132
  4.2 41.1 %all_to_all.10 = bf16[64,8,896]{2,1,0:T(8,128)(2,1)S(1)} all-to-all(bf16[64,8,896]{2,1,0:T(8,128)(2,1)S(1)} %sort_rows.1), channel_id=1, replica_groups=mesh['z'=8,'x'=4,'c'=2,'t'=8] {'z','t'}, dimensions={0} | all-to-all | bytes 1835008 | tf_op jit(solution)/shard_map/all_to_all | solution.py:140
  45.3 0.1 slice_bitcast_fusion
  45.3 0.9 copy.9
  46.2 7.4 %all-to-all-start.1 = ((bf16[8,64,640]{2,1,0:T(8,128)(2,1)}), bf16[8,64,640]{2,1,0:T(8,128)(2,1)S(1)}, u32[]{:S(2)}, u32[]{:S(2)}) async-start(bf16[8,64,640]{2,1,0:T(8,128)(2,1)} %copy.9), calls=%async_computation.1 | async-start | bytes 1310720 | tf_op jit(solution)/shard_map/all_to_all | solution.py:145
  53.6 0.0 copy-start.2
  53.7 0.0 copy-start.4
  53.7 0.0 copy-start.5
  53.7 2.5 %collective-permute-start.2 = (bf16[8,64,256]{2,1,0:T(8,128)(2,1)S(1)}, bf16[8,64,256]{2,1,0:T(8,128)(2,1)S(1)}, u32[]{:S(2)}, u32[]{:S(2)}) collective-permute-start(bf16[8,64,256]{2,1,0:T(8,128)(2,1)S(1)} %bitcast.12), channel_id=1, source_target_pairs={{0,48},{16,0},{32,16},{48,32},{1,49},{17,1},{33,17},{49,33},{2,50}... | collective-permute-start | bytes 786440 | tf_op jit(solution)/shard_map/ppermute | solution.py:124
  56.2 2.6 %collective-permute-start.1 = (bf16[8,64,256]{2,1,0:T(8,128)(2,1)S(1)}, bf16[8,64,256]{2,1,0:T(8,128)(2,1)S(1)}, u32[]{:S(2)}, u32[]{:S(2)}) collective-permute-start(bf16[8,64,256]{2,1,0:T(8,128)(2,1)S(1)} %bitcast.13), channel_id=1, source_target_pairs={{0,32},{16,48},{32,0},{48,16},{1,33},{17,49},{33,1},{49,17},{2,34}... | collective-permute-start | bytes 786440 | tf_op jit(solution)/shard_map/ppermute | solution.py:124
  58.8 3.9 %collective-permute-start = (bf16[8,64,256]{2,1,0:T(8,128)(2,1)S(1)}, bf16[8,64,256]{2,1,0:T(8,128)(2,1)S(1)}, u32[]{:S(2)}, u32[]{:S(2)}) collective-permute-start(bf16[8,64,256]{2,1,0:T(8,128)(2,1)S(1)} %bitcast.14), channel_id=1, source_target_pairs={{0,16},{16,32},{32,48},{48,0},{1,17},{17,33},{33,49},{49,1},{2,18}... | collective-permute-start | bytes 786440 | tf_op jit(solution)/shard_map/ppermute | solution.py:124
  62.7 3.1 %collective-permute-start.3 = (bf16[8,64,256]{2,1,0:T(8,128)(2,1)S(1)}, bf16[8,64,256]{2,1,0:T(8,128)(2,1)S(1)}, u32[]{:S(2)}, u32[]{:S(2)}) collective-permute-start(bf16[8,64,256]{2,1,0:T(8,128)(2,1)S(1)} %bitcast.15), channel_id=1, source_target_pairs={{0,8},{8,0},{1,9},{9,1},{2,10},{10,2},{3,11},{11,3},{4,12},{12,4},... | collective-permute-start | bytes 786440 | tf_op jit(solution)/shard_map/ppermute | solution.py:124
  65.9 1.2 %collective-permute-done.2.a3 = bf16[8,64,256]{2,1,0:T(8,128)(2,1)S(1)} collective-permute-done((bf16[8,64,256]{2,1,0:T(8,128)(2,1)S(1)}, bf16[8,64,256]{2,1,0:T(8,128)(2,1)S(1)}, u32[]{:S(2)}, u32[]{:S(2)}) %collective-permute-start.2) | collective-permute-done | bytes 262176 | tf_op jit(solution)/shard_map/ppermute | solution.py:124
  67.1 3.0 %collective-permute-start.6 = (bf16[8,64,256]{2,1,0:T(8,128)(2,1)S(1)}, bf16[8,64,256]{2,1,0:T(8,128)(2,1)S(1)}, u32[]{:S(2)}, u32[]{:S(2)}) collective-permute-start(bf16[8,64,256]{2,1,0:T(8,128)(2,1)S(1)} %collective-permute-done.2.a3), channel_id=1, source_target_pairs={{0,8},{8,0},{1,9},{9,1},{2,10},{10,2},{3,11},{11,3},{4,12},{12,4},... | collective-permute-start | bytes 786440 | tf_op jit(solution)/shard_map/ppermute | solution.py:124
  70.1 4.0 %collective-permute-done.1.a2 = bf16[8,64,256]{2,1,0:T(8,128)(2,1)S(1)} collective-permute-done((bf16[8,64,256]{2,1,0:T(8,128)(2,1)S(1)}, bf16[8,64,256]{2,1,0:T(8,128)(2,1)S(1)}, u32[]{:S(2)}, u32[]{:S(2)}) %collective-permute-start.1) | collective-permute-done | bytes 262176 | tf_op jit(solution)/shard_map/ppermute | solution.py:124
  74.1 2.8 %collective-permute-start.5 = (bf16[8,64,256]{2,1,0:T(8,128)(2,1)S(1)}, bf16[8,64,256]{2,1,0:T(8,128)(2,1)S(1)}, u32[]{:S(2)}, u32[]{:S(2)}) collective-permute-start(bf16[8,64,256]{2,1,0:T(8,128)(2,1)S(1)} %collective-permute-done.1.a2), channel_id=1, source_target_pairs={{0,8},{8,0},{1,9},{9,1},{2,10},{10,2},{3,11},{11,3},{4,12},{12,4},... | collective-permute-start | bytes 786440 | tf_op jit(solution)/shard_map/ppermute | solution.py:124
  76.9 0.0 collective-permute-done.a1
  76.9 1.9 %collective-permute-start.4 = (bf16[8,64,256]{2,1,0:T(8,128)(2,1)S(1)}, bf16[8,64,256]{2,1,0:T(8,128)(2,1)S(1)}, u32[]{:S(2)}, u32[]{:S(2)}) collective-permute-start(bf16[8,64,256]{2,1,0:T(8,128)(2,1)S(1)} %collective-permute-done.a1), channel_id=1, source_target_pairs={{0,8},{8,0},{1,9},{9,1},{2,10},{10,2},{3,11},{11,3},{4,12},{12,4},... | collective-permute-start | bytes 786440 | tf_op jit(solution)/shard_map/ppermute | solution.py:124
  78.8 0.0 collective-permute-done.3.b0
  78.8 0.0 collective-permute-done.6.b3
  78.8 0.0 collective-permute-done.5.b2
  78.8 1.5 %collective-permute-done.4.b1 = bf16[8,64,256]{2,1,0:T(8,128)(2,1)S(1)} collective-permute-done((bf16[8,64,256]{2,1,0:T(8,128)(2,1)S(1)}, bf16[8,64,256]{2,1,0:T(8,128)(2,1)S(1)}, u32[]{:S(2)}, u32[]{:S(2)}) %collective-permute-start.4) | collective-permute-done | bytes 262176 | tf_op jit(solution)/shard_map/ppermute | solution.py:124
  80.3 0.0 all-to-all-done.1
  80.3 0.0 copy-done.2
  80.3 0.0 copy-done.4
  80.3 0.0 copy-done.5
  80.3 14.4 %tree_attention.1 = bf16[512,640]{1,0:T(8,128)(2,1)} custom-call(s32[4]{0:T(128)S(1)} %pad_add_fusion.place, s32[4,10]{1,0:T(4,128)S(1)} %copy-done.4, s32[4]{0:T(128)S(1)} %copy-done.5, s32[256,128]{1,0:T(8,128)S(1)} %bitcast.18, bf16[512,640]{1,0:T(8,128)(2,1)S(1)} %bitcast.11, bf16[8,64,256]{2,1,0:T(8,128)(2,1)S(1)} %bitcast.16, ...), custom_call_target="tpu_custom_call" | custom-call | tf_op jit(solution)/shard_map/tree_attention/pallas_call | solution.py:146
  (2 shorter events, 0.1 us)
Async XLA Ops:
  0.1 1.1 %copy-start = (bf16[64,5120]{1,0:T(8,128)(2,1)S(1)}, bf16[64,5120]{1,0:T(8,128)(2,1)}, u32[]{:S(2)}) copy-start(bf16[64,5120]{1,0:T(8,128)(2,1)} %query.1) | copy-start | bytes 1966084
  1.2 0.9 copy-start.1
  2.1 0.9 %copy-start.3 = (bf16[64,2048]{1,0:T(8,128)(2,1)S(1)}, bf16[64,2048]{1,0:T(8,128)(2,1)}, u32[]{:S(2)}) copy-start(bf16[64,2048]{1,0:T(8,128)(2,1)} %pairs.1) | copy-start | bytes 786436
  46.2 34.1 %all-to-all-start.1 = ((bf16[8,64,640]{2,1,0:T(8,128)(2,1)}), bf16[8,64,640]{2,1,0:T(8,128)(2,1)S(1)}, u32[]{:S(2)}, u32[]{:S(2)}) async-start(bf16[8,64,640]{2,1,0:T(8,128)(2,1)} %copy.9), calls=%async_computation.1 | async-start | bytes 1310720 | tf_op jit(solution)/shard_map/all_to_all | solution.py:145
  53.6 26.7 %copy-start.2 = (s32[32768]{0:T(1024)S(1)}, s32[32768]{0:T(1024)}, u32[]{:S(2)}) copy-start(s32[32768]{0:T(1024)} %param.7) | copy-start | bytes 393220
  53.7 26.6 %copy-start.4 = (s32[4,10]{1,0:T(4,128)S(1)}, s32[4,10]{1,0:T(4,128)}, u32[]{:S(2)}) copy-start(s32[4,10]{1,0:T(4,128)} %ancestors.1) | copy-start | bytes 484
  53.7 26.6 %copy-start.5 = (s32[4]{0:T(128)S(1)}, s32[4]{0:T(128)}, u32[]{:S(2)}) copy-start(s32[4]{0:T(128)} %depth.1) | copy-start | bytes 52
  53.7 13.3 %collective-permute-start.2 = (bf16[8,64,256]{2,1,0:T(8,128)(2,1)S(1)}, bf16[8,64,256]{2,1,0:T(8,128)(2,1)S(1)}, u32[]{:S(2)}, u32[]{:S(2)}) collective-permute-start(bf16[8,64,256]{2,1,0:T(8,128)(2,1)S(1)} %bitcast.12), channel_id=1, source_target_pairs={{0,48},{16,0},{32,16},{48,32},{1,49},{17,1},{33,17},{49,33},{2,50}... | collective-permute-start | bytes 786440 | tf_op jit(solution)/shard_map/ppermute | solution.py:124
  56.2 17.8 %collective-permute-start.1 = (bf16[8,64,256]{2,1,0:T(8,128)(2,1)S(1)}, bf16[8,64,256]{2,1,0:T(8,128)(2,1)S(1)}, u32[]{:S(2)}, u32[]{:S(2)}) collective-permute-start(bf16[8,64,256]{2,1,0:T(8,128)(2,1)S(1)} %bitcast.13), channel_id=1, source_target_pairs={{0,32},{16,48},{32,0},{48,16},{1,33},{17,49},{33,1},{49,17},{2,34}... | collective-permute-start | bytes 786440 | tf_op jit(solution)/shard_map/ppermute | solution.py:124
  58.8 18.0 %collective-permute-start = (bf16[8,64,256]{2,1,0:T(8,128)(2,1)S(1)}, bf16[8,64,256]{2,1,0:T(8,128)(2,1)S(1)}, u32[]{:S(2)}, u32[]{:S(2)}) collective-permute-start(bf16[8,64,256]{2,1,0:T(8,128)(2,1)S(1)} %bitcast.14), channel_id=1, source_target_pairs={{0,16},{16,32},{32,48},{48,0},{1,17},{17,33},{33,49},{49,1},{2,18}... | collective-permute-start | bytes 786440 | tf_op jit(solution)/shard_map/ppermute | solution.py:124
  62.7 16.1 %collective-permute-start.3 = (bf16[8,64,256]{2,1,0:T(8,128)(2,1)S(1)}, bf16[8,64,256]{2,1,0:T(8,128)(2,1)S(1)}, u32[]{:S(2)}, u32[]{:S(2)}) collective-permute-start(bf16[8,64,256]{2,1,0:T(8,128)(2,1)S(1)} %bitcast.15), channel_id=1, source_target_pairs={{0,8},{8,0},{1,9},{9,1},{2,10},{10,2},{3,11},{11,3},{4,12},{12,4},... | collective-permute-start | bytes 786440 | tf_op jit(solution)/shard_map/ppermute | solution.py:124
  67.1 11.7 %collective-permute-start.6 = (bf16[8,64,256]{2,1,0:T(8,128)(2,1)S(1)}, bf16[8,64,256]{2,1,0:T(8,128)(2,1)S(1)}, u32[]{:S(2)}, u32[]{:S(2)}) collective-permute-start(bf16[8,64,256]{2,1,0:T(8,128)(2,1)S(1)} %collective-permute-done.2.a3), channel_id=1, source_target_pairs={{0,8},{8,0},{1,9},{9,1},{2,10},{10,2},{3,11},{11,3},{4,12},{12,4},... | collective-permute-start | bytes 786440 | tf_op jit(solution)/shard_map/ppermute | solution.py:124
  74.1 4.7 %collective-permute-start.5 = (bf16[8,64,256]{2,1,0:T(8,128)(2,1)S(1)}, bf16[8,64,256]{2,1,0:T(8,128)(2,1)S(1)}, u32[]{:S(2)}, u32[]{:S(2)}) collective-permute-start(bf16[8,64,256]{2,1,0:T(8,128)(2,1)S(1)} %collective-permute-done.1.a2), channel_id=1, source_target_pairs={{0,8},{8,0},{1,9},{9,1},{2,10},{10,2},{3,11},{11,3},{4,12},{12,4},... | collective-permute-start | bytes 786440 | tf_op jit(solution)/shard_map/ppermute | solution.py:124
  76.9 3.4 %collective-permute-start.4 = (bf16[8,64,256]{2,1,0:T(8,128)(2,1)S(1)}, bf16[8,64,256]{2,1,0:T(8,128)(2,1)S(1)}, u32[]{:S(2)}, u32[]{:S(2)}) collective-permute-start(bf16[8,64,256]{2,1,0:T(8,128)(2,1)S(1)} %collective-permute-done.a1), channel_id=1, source_target_pairs={{0,8},{8,0},{1,9},{9,1},{2,10},{10,2},{3,11},{11,3},{4,12},{12,4},... | collective-permute-start | bytes 786440 | tf_op jit(solution)/shard_map/ppermute | solution.py:124

commit v2 on v1

v2 whole, which is shorter than its diff:
```python
import functools
import math

import jax
import jax.numpy as jnp
from jax import lax
from jax.experimental import pallas as pl
from jax.experimental.pallas import tpu as pltpu
from jax.sharding import Mesh
from jax.sharding import PartitionSpec as P

HEAD = 128
BLOCK = 128
SLOTS = 10
GROUP = 5
KEYS = (SLOTS + 1) * BLOCK
NEG = -1e30
VMEM_LIMIT = 24 * 1024 * 1024
NT = (((1,), (1,)), ((), ()))


def one_hot(hit):
    return jnp.where(hit, 1.0, 0.0).astype(jnp.bfloat16)


def iota(shape, dim):
    return lax.broadcasted_iota(jnp.int32, shape, dim)


def sort_kernel(index_hbm, query_hbm, pairs_hbm, out, index, query, pairs, sems):
    copies = [
        pltpu.make_async_copy(src, dst, sems.at[k])
        for k, (src, dst) in enumerate(((index_hbm, index), (pairs_hbm, pairs), (query_hbm, query)))
    ]
    for copy in copies:
        copy.start()
    z, x, c, t = (lax.axis_index(n) for n in ("z", "x", "c", "t"))
    device = ((z * 4 + x) * 2 + c) * 8 + t
    group = one_hot((iota((64, 256), 1) >> 2) == iota((64, 256), 0))
    copies[0].wait()
    idx = index[...]
    local = jnp.where((idx >> 6) == device, (idx & 63).astype(jnp.float32), 0.0).astype(jnp.bfloat16)
    source = jnp.sum(jnp.dot(group, local, preferred_element_type=jnp.float32), 1, keepdims=True)
    picker = one_hot(source.astype(jnp.int32) == iota((64, 64), 1))
    copies[1].wait()
    copies[2].wait()
    for t in range(8):
        q = jnp.dot(picker, query[:, t * 640 : (t + 1) * 640], preferred_element_type=jnp.float32)
        kv = jnp.dot(picker, pairs[:, t * 256 : (t + 1) * 256], preferred_element_type=jnp.float32)
        for z in range(8):
            out[z * 8 + t, :, :640] = q[z * 8 : (z + 1) * 8].astype(jnp.bfloat16)
            out[z * 8 + t, :, 640:] = kv[z * 8 : (z + 1) * 8].astype(jnp.bfloat16)


def regroup_kernel(landed, ahead, back, mate, keep, parts):
    x, c = lax.axis_index("x"), lax.axis_index("c")
    want, have = iota((128, 128), 0), iota((128, 128), 1)
    turn = one_hot(((want >> 4) == (have & 7)) & ((want & 15) == (have >> 3)))
    for k in range(4):
        rows = slice(k * 16, (k + 1) * 16)
        got = jnp.dot(turn, landed[rows].reshape(128, 896), preferred_element_type=jnp.float32)
        got = got.astype(jnp.bfloat16)
        for shard in range(8):
            piece = got[shard * 16 : (shard + 1) * 16]
            for h in range(GROUP):
                parts[shard, h, rows, :] = piece[:, h * 128 : (h + 1) * 128]
            for e in range(2):
                pair = piece[:, 640 + e * 128 : 768 + e * 128]
                ahead[10 + shard * 2 + e, rows, :] = pair
                back[shard * 2 + e, rows, :] = pair
                mate[shard * 2 + e, rows, :] = pair
    way = 1 - 2 * c

    def part(step, core):
        return parts[((x + step) & 3) * 2 + (c ^ core)]

    ahead[0:5] = part(2, 0)
    ahead[5:10] = part(2, 1)
    ahead[26:31] = part(way, 1)
    ahead[31:36] = part(way, 0)
    back[16:21] = part(-way, 1)
    back[21:26] = part(-way, 0)
    mate[16:21] = part(0, 1)
    keep[...] = part(0, 0)


def arrival(idx, in_tree):
    source = idx >> 6
    behind = ((in_tree >> 1) - (source >> 4)) & 3
    behind = jnp.where((source & 8) != 0, (4 - behind) & 3, behind)
    order = jnp.where(behind == 2, 3, jnp.where(behind == 3, 2, behind))
    other = ((source >> 3) ^ in_tree) & 1
    return (other << 8) | (order << 6) | ((source >> 6) << 3) | (source & 7)


def picker_of(pos_row):
    column = jnp.transpose(jnp.broadcast_to(pos_row.astype(jnp.float32), (128, 128)))
    parts = []
    for k in range(4):
        lane = (lax.broadcasted_iota(jnp.int32, (128, 128), 1) + k * 128).astype(jnp.float32)
        parts.append(jnp.where(column == lane, 1.0, 0.0).astype(jnp.bfloat16))
    return jnp.concatenate(parts, 1)


def attend_kernel(
    ancestors, depth, index, keep, own, near, far, across, mate, first, rest, out,
    keys, values, local_q, kc, vc, scores, probs,
):
    z, in_tree = lax.axis_index("z"), lax.axis_index("x") * 2 + lax.axis_index("c")
    slabs = ((own, 0), (near, 10), (far, 0), (across, 10), (mate, 0), (first, 0), (rest, 0), (rest, 26))
    parts = ((keep, 0), (near, 31), (far, 21), (across, 0), (mate, 16), (first, 16), (rest, 16), (rest, 21))

    def picked(block, raw):
        pick = picker_of(arrival(index[pl.ds(z * 32 + block, 1), :], in_tree))
        return jnp.dot(pick, raw, preferred_element_type=jnp.float32).astype(jnp.bfloat16)

    def place_shard(j, carry):
        raw = jnp.concatenate(
            [jnp.concatenate([r[base + 2 * j + e] for r, base in slabs], 0) for e in range(2)], 1
        )
        for n in range(4):
            got = picked(j * 4 + n, raw)
            keys[j * 4 + n] = got[:, :128]
            values[j * 4 + n] = got[:, 128:]
        return carry

    lax.fori_loop(0, in_tree + 1, place_shard, 0)
    raw = jnp.concatenate(
        [jnp.concatenate([r[base + h] for r, base in parts], 0) for h in range(GROUP)], 1
    )
    for n in range(4):
        got = picked(in_tree * 4 + n, raw)
        for h in range(GROUP):
            local_q[n, h * 128 : (h + 1) * 128, :] = got[:, h * 128 : (h + 1) * 128]
    vc[:, 128:] = jnp.ones((KEYS, 128), jnp.bfloat16)
    factor = math.log2(math.e) / math.sqrt(HEAD)

    def attend(b, carry):
        levels = depth[b]
        for j in range(SLOTS):
            block = ancestors[b, j] - z * 32
            kc[j * 128 : (j + 1) * 128, :] = keys[block]
            vc[j * 128 : (j + 1) * 128, :128] = values[block]
        me = in_tree * 4 + b
        kc[SLOTS * 128 :, :] = keys[me]
        vc[SLOTS * 128 :, :128] = values[me]
        scores[...] = lax.dot_general(local_q[b], kc[...], NT, preferred_element_type=jnp.float32)
        slot = lax.broadcasted_iota(jnp.int32, (1, SLOTS * 128), 1) >> 7
        bias = jnp.where(slot < levels, 0.0, NEG)
        r = lax.broadcasted_iota(jnp.int32, (128, 128), 0)
        n = lax.broadcasted_iota(jnp.int32, (128, 128), 1)
        causal = jnp.where(n <= r, 0.0, NEG)
        for h in range(GROUP):
            rows = slice(h * 128, (h + 1) * 128)
            s0 = scores[rows, : SLOTS * 128] + bias
            s1 = scores[rows, SLOTS * 128 :] + causal
            top = jnp.maximum(jnp.max(s0, 1, keepdims=True), jnp.max(s1, 1, keepdims=True))
            probs[rows, : SLOTS * 128] = jnp.exp2((s0 - top) * factor).astype(jnp.bfloat16)
            probs[rows, SLOTS * 128 :] = jnp.exp2((s1 - top) * factor).astype(jnp.bfloat16)
        acc = jnp.dot(probs[...], vc[...], preferred_element_type=jnp.float32)
        res = (acc[:, :128] / acc[:, 128:]).astype(jnp.bfloat16)
        for h in range(GROUP):
            out[pl.ds(pl.multiple_of(b * 128, 128), 128), h * 128 : (h + 1) * 128] = res[h * 128 : (h + 1) * 128]
        return carry

    lax.fori_loop(0, 4, attend, 0)


SMEM = pl.BlockSpec(memory_space=pltpu.SMEM)
HBM = pl.BlockSpec(memory_space=pltpu.HBM)
VMEM = pl.BlockSpec(memory_space=pltpu.VMEM)


def ring(block, way):
    route = [(x * 2 + c, (x + (way if c == 0 else -way)) % 4 * 2 + c) for x in range(4) for c in range(2)]
    return lax.ppermute(block, ("x", "c"), route)


def swap(block):
    return lax.ppermute(block, "c", [(0, 1), (1, 0)])


def exchange(block, axes):
    return lax.all_to_all(block, axes, split_axis=0, concat_axis=0, tiled=True)


def finish(ancestors, depth, index, *tiles):
    return pl.pallas_call(
        attend_kernel,
        out_shape=jax.ShapeDtypeStruct((512, 640), jnp.bfloat16),
        in_specs=[SMEM] * 2 + [VMEM] * 9,
        out_specs=VMEM,
        scratch_shapes=[
            pltpu.VMEM((32, 128, 128), jnp.bfloat16),
            pltpu.VMEM((32, 128, 128), jnp.bfloat16),
            pltpu.VMEM((4, 640, 128), jnp.bfloat16),
            pltpu.VMEM((KEYS, 128), jnp.bfloat16),
            pltpu.VMEM((KEYS, 256), jnp.bfloat16),
            pltpu.VMEM((640, KEYS), jnp.float32),
            pltpu.VMEM((640, KEYS), jnp.bfloat16),
        ],
        compiler_params=pltpu.CompilerParams(vmem_limit_bytes=VMEM_LIMIT),
        name="tree_attention",
    )(ancestors, depth, index, *tiles)


def body(query_beam, key_value_beam, beam_row_index, ancestors, depth):
    index = beam_row_index.reshape(256, 128)
    bf16 = jnp.bfloat16
    packed = pl.pallas_call(
        sort_kernel,
        out_shape=jax.ShapeDtypeStruct((64, 8, 896), bf16),
        in_specs=[HBM] * 3,
        out_specs=VMEM,
        scratch_shapes=[
            pltpu.VMEM((256, 128), jnp.int32),
            pltpu.VMEM((64, 5120), bf16),
            pltpu.VMEM((64, 2048), bf16),
            pltpu.SemaphoreType.DMA((3,)),
        ],
        name="sort_rows",
    )(index, query_beam, key_value_beam)
    landed = exchange(packed, ("z", "t"))
    params = pltpu.CompilerParams(vmem_limit_bytes=VMEM_LIMIT)
    ahead, back, mate, keep = pl.pallas_call(
        regroup_kernel,
        out_shape=[jax.ShapeDtypeStruct((n, 64, 128), bf16) for n in (36, 26, 21, 5)],
        in_specs=[VMEM],
        out_specs=[VMEM] * 4,
        scratch_shapes=[pltpu.VMEM((8, GROUP, 64, 128), bf16)],
        compiler_params=params,
        name="regroup",
    )(landed)
    near = ring(ahead, 1)
    far = ring(back, -1)
    mate_swapped = swap(mate)
    near, mate_swapped = lax.optimization_barrier((near, mate_swapped))
    across = ring(near[:26], 1)
    first = swap(near[10:31])
    far, first = lax.optimization_barrier((far, first))
    rest = swap(jnp.concatenate([far[:21], across[5:]], 0))
    return finish(ancestors, depth, index, keep, mate, near, far, across, mate_swapped, first, rest)


def solution(mesh):
    fine = Mesh(mesh.devices.reshape(8, 4, 2, 8), ("z", "x", "c", "t"))
    every, shard = ("z", "x", "c", "t"), ("z", "x", "c")
    return jax.shard_map(
        body,
        mesh=fine,
        in_specs=(P(every, None), P(every, None), P(), P(shard, None), P(shard)),
        out_specs=P(shard, "t"),
        check_vma=False,
    )
```

time: 95.2 us -> 91.3 us (0.959)
  the two profiles are of different devices: /device:TPU:7 before, /device:TPU:1 now
where the time goes in v2:
time: 91.3 us; the launch traced here: 90.9 us
  blocking collectives  42.1 us (46%)
  starting transfers between devices  29.2 us (32%)
  Pallas kernels  15.2 us (17%)
  waiting for transfers between devices  2.99 us (3%)
  local copies, waits for them, and re-layouts  1.05 us (1%)
    all_to_all x1, blocking collectives, exchange(): return lax.all_to_all(block, axes, split_axis=0, concat_axis=0, tiled=True)  42.1 us
    ppermute x3, starting transfers between devices, swap(): return lax.ppermute(block, 'c', [(0, 1), (1, 0)])  17 us
    ppermute x3, starting transfers between devices, ring(): return lax.ppermute(block, ('x', 'c'), route)  12.2 us
    pallas_call x1, Pallas kernels, finish(): pl.pallas_call(attend_kernel, out_shape=jax.ShapeDtypeStruct((512, 640),...  12.2 us
    ppermute x3, waiting for transfers between devices, swap(): return lax.ppermute(block, 'c', [(0, 1), (1, 0)])  2.99 us
    pallas_call x1, Pallas kernels, body(): pl.pallas_call(sort_kernel, out_shape=jax.ShapeDtypeStruct((64, 8, 896),...  2.58 us
  transfers between devices with their start and end apart: 6, of which 2 were waited for; matrix products, arithmetic and copies ran while one was open for 0% of the time, Pallas kernels for 0%

profile of v2, /device:TPU:1, one launch (start us, length us, event | category | flops | bytes accessed | tf_op | source)
XLA Modules:
  0.0 90.9 jit_solution(16612690830586391441)
XLA Ops:
  0.0 2.6 %sort_rows.1 = bf16[64,8,896]{2,1,0:T(8,128)(2,1)} custom-call(s32[256,128]{1,0:T(8,128)} %bitcast.1, bf16[64,5120]{1,0:T(8,128)(2,1)} %query_hbm.1, bf16[64,2048]{1,0:T(8,128)(2,1)} %pairs_hbm.1), custom_call_target="tpu_custom_call" | custom-call | tf_op jit(solution)/shard_map/sort_rows/pallas_call | solution.py:210
  2.6 42.1 %all_to_all.5.landed = bf16[64,8,896]{2,1,0:T(8,128)(2,1)S(1)} all-to-all(bf16[64,8,896]{2,1,0:T(8,128)(2,1)} %sort_rows.1), channel_id=1, replica_groups=mesh['z'=8,'x'=4,'c'=2,'t'=8] {'z','t'}, dimensions={0} | all-to-all | bytes 1835008 | tf_op jit(solution)/shard_map/all_to_all | solution.py:184
  44.7 0.4 regroup.1
  45.2 4.4 %collective-permute-start = (bf16[36,64,128]{2,1,0:T(8,128)(2,1)S(1)}, bf16[36,64,128]{2,1,0:T(8,128)(2,1)S(1)}, u32[]{:S(2)}, u32[]{:S(2)}) collective-permute-start(bf16[36,64,128]{2,1,0:T(8,128)(2,1)S(1)} %get-tuple-element.15), channel_id=1, source_target_pairs={{0,16},{8,56},{16,32},{24,8},{32,48},{40,24},{48,0},{56,40},{1,17}... | collective-permute-start | bytes 1769480 | tf_op jit(solution)/shard_map/ppermute | solution.py:176
  49.5 3.9 %collective-permute-start.1 = (bf16[21,64,128]{2,1,0:T(8,128)(2,1)S(1)}, bf16[21,64,128]{2,1,0:T(8,128)(2,1)S(1)}, u32[]{:S(2)}, u32[]{:S(2)}) collective-permute-start(bf16[21,64,128]{2,1,0:T(8,128)(2,1)S(1)} %get-tuple-element.14.own), channel_id=1, source_target_pairs={{0,8},{8,0},{1,9},{9,1},{2,10},{10,2},{3,11},{11,3},{4,12},{12,4},... | collective-permute-start | bytes 1032200 | tf_op jit(solution)/shard_map/ppermute | solution.py:180
  53.5 3.1 %collective-permute-start.2 = (bf16[26,64,128]{2,1,0:T(8,128)(2,1)S(1)}, bf16[26,64,128]{2,1,0:T(8,128)(2,1)S(1)}, u32[]{:S(2)}, u32[]{:S(2)}) collective-permute-start(bf16[26,64,128]{2,1,0:T(8,128)(2,1)S(1)} %get-tuple-element.17), channel_id=1, source_target_pairs={{0,48},{8,24},{16,0},{24,40},{32,16},{40,56},{48,32},{56,8},{1,49}... | collective-permute-start | bytes 1277960 | tf_op jit(solution)/shard_map/ppermute | solution.py:176
  56.6 0.0 collective-permute-done.1.mate
  56.6 0.0 collective-permute-done.near
  56.6 4.8 %collective-permute-start.4 = (bf16[26,64,128]{2,1,0:T(8,128)(2,1)S(1)}, bf16[26,64,128]{2,1,0:T(8,128)(2,1)S(1)}, u32[]{:S(2)}, u32[]{:S(2)}) collective-permute-start(bf16[26,64,128]{2,1,0:T(8,128)(2,1)S(1)} %slice.13), channel_id=1, source_target_pairs={{0,16},{8,56},{16,32},{24,8},{32,48},{40,24},{48,0},{56,40},{1,17}... | collective-permute-start | bytes 1277960 | tf_op jit(solution)/shard_map/ppermute | solution.py:176
  61.4 5.2 %collective-permute-start.3 = (bf16[21,64,128]{2,1,0:T(8,128)(2,1)S(1)}, bf16[21,64,128]{2,1,0:T(8,128)(2,1)S(1)}, u32[]{:S(2)}, u32[]{:S(2)}) collective-permute-start(bf16[21,64,128]{2,1,0:T(8,128)(2,1)S(1)} %slice.12), channel_id=1, source_target_pairs={{0,8},{8,0},{1,9},{9,1},{2,10},{10,2},{3,11},{11,3},{4,12},{12,4},... | collective-permute-start | bytes 1032200 | tf_op jit(solution)/shard_map/ppermute | solution.py:180
  66.7 0.0 collective-permute-done.2.far
  66.7 0.0 copy-start
  66.7 1.2 %collective-permute-done.3.first = bf16[21,64,128]{2,1,0:T(8,128)(2,1)S(1)} collective-permute-done((bf16[21,64,128]{2,1,0:T(8,128)(2,1)S(1)}, bf16[21,64,128]{2,1,0:T(8,128)(2,1)S(1)}, u32[]{:S(2)}, u32[]{:S(2)}) %collective-permute-start.3) | collective-permute-done | bytes 344096 | tf_op jit(solution)/shard_map/ppermute | solution.py:180
  67.9 0.0 copy-done
  68.0 0.0 collective-permute-done.4.across
  68.0 0.0 slice-start
  68.0 0.9 %slice-done = bf16[21,64,128]{2,1,0:T(8,128)(2,1)S(1)} async-done(((bf16[26,64,128]{2,1,0:T(8,128)(2,1)}), bf16[21,64,128]{2,1,0:T(8,128)(2,1)S(1)}, s32[]{:S(2)}) %slice-start) | async-done | bytes 344088 | tf_op jit(solution)/shard_map/slice | solution.py:241
  68.9 0.0 copy-start.1
  68.9 0.0 copy-start.2
  68.9 0.0 copy-start.3
  68.9 0.1 pad_maximum_fusion
  69.0 0.0 copy-start.4
  69.0 7.9 %collective-permute-start.5 = (bf16[42,64,128]{2,1,0:T(8,128)(2,1)S(1)}, bf16[42,64,128]{2,1,0:T(8,128)(2,1)S(1)}, u32[]{:S(2)}, u32[]{:S(2)}) collective-permute-start(bf16[42,64,128]{2,1,0:T(8,128)(2,1)S(1)} %pad_maximum_fusion), channel_id=1, source_target_pairs={{0,8},{8,0},{1,9},{9,1},{2,10},{10,2},{3,11},{11,3},{4,12},{12,4},... | collective-permute-start | bytes 2064392 | tf_op jit(solution)/shard_map/ppermute | solution.py:180
  76.9 1.7 %collective-permute-done.5.rest = bf16[42,64,128]{2,1,0:T(8,128)(2,1)S(1)} collective-permute-done((bf16[42,64,128]{2,1,0:T(8,128)(2,1)S(1)}, bf16[42,64,128]{2,1,0:T(8,128)(2,1)S(1)}, u32[]{:S(2)}, u32[]{:S(2)}) %collective-permute-start.5) | collective-permute-done | bytes 688160 | tf_op jit(solution)/shard_map/ppermute | solution.py:180
  78.6 0.0 copy-done.1
  78.6 0.0 copy-done.2
  78.6 0.0 copy-done.3
  78.6 0.0 copy-done.4
  78.6 12.2 %tree_attention.1 = bf16[512,640]{1,0:T(8,128)(2,1)} custom-call(s32[4,10]{1,0:T(4,128)S(1)} %copy-done.3, s32[4]{0:T(128)S(1)} %copy-done.4, s32[256,128]{1,0:T(8,128)S(1)} %bitcast.2, bf16[5,64,128]{2,1,0:T(8,128)(2,1)S(1)} %get-tuple-element.13.keep, bf16[21,64,128]{2,1,0:T(8,128)(2,1)S(1)} %get-tuple-element.14.own, ...), custom_call_target="tpu_custom_call" | custom-call | tf_op jit(solution)/shard_map/tree_attention/pallas_call | solution.py:188
  (3 shorter events, 0.1 us)
Async XLA Ops:
  45.2 11.4 %collective-permute-start = (bf16[36,64,128]{2,1,0:T(8,128)(2,1)S(1)}, bf16[36,64,128]{2,1,0:T(8,128)(2,1)S(1)}, u32[]{:S(2)}, u32[]{:S(2)}) collective-permute-start(bf16[36,64,128]{2,1,0:T(8,128)(2,1)S(1)} %get-tuple-element.15), channel_id=1, source_target_pairs={{0,16},{8,56},{16,32},{24,8},{32,48},{40,24},{48,0},{56,40},{1,17}... | collective-permute-start | bytes 1769480 | tf_op jit(solution)/shard_map/ppermute | solution.py:176
  49.5 7.1 %collective-permute-start.1 = (bf16[21,64,128]{2,1,0:T(8,128)(2,1)S(1)}, bf16[21,64,128]{2,1,0:T(8,128)(2,1)S(1)}, u32[]{:S(2)}, u32[]{:S(2)}) collective-permute-start(bf16[21,64,128]{2,1,0:T(8,128)(2,1)S(1)} %get-tuple-element.14.own), channel_id=1, source_target_pairs={{0,8},{8,0},{1,9},{9,1},{2,10},{10,2},{3,11},{11,3},{4,12},{12,4},... | collective-permute-start | bytes 1032200 | tf_op jit(solution)/shard_map/ppermute | solution.py:180
  53.5 13.2 %collective-permute-start.2 = (bf16[26,64,128]{2,1,0:T(8,128)(2,1)S(1)}, bf16[26,64,128]{2,1,0:T(8,128)(2,1)S(1)}, u32[]{:S(2)}, u32[]{:S(2)}) collective-permute-start(bf16[26,64,128]{2,1,0:T(8,128)(2,1)S(1)} %get-tuple-element.17), channel_id=1, source_target_pairs={{0,48},{8,24},{16,0},{24,40},{32,16},{40,56},{48,32},{56,8},{1,49}... | collective-permute-start | bytes 1277960 | tf_op jit(solution)/shard_map/ppermute | solution.py:176
  56.6 11.3 %collective-permute-start.4 = (bf16[26,64,128]{2,1,0:T(8,128)(2,1)S(1)}, bf16[26,64,128]{2,1,0:T(8,128)(2,1)S(1)}, u32[]{:S(2)}, u32[]{:S(2)}) collective-permute-start(bf16[26,64,128]{2,1,0:T(8,128)(2,1)S(1)} %slice.13), channel_id=1, source_target_pairs={{0,16},{8,56},{16,32},{24,8},{32,48},{40,24},{48,0},{56,40},{1,17}... | collective-permute-start | bytes 1277960 | tf_op jit(solution)/shard_map/ppermute | solution.py:176
  61.4 6.5 %collective-permute-start.3 = (bf16[21,64,128]{2,1,0:T(8,128)(2,1)S(1)}, bf16[21,64,128]{2,1,0:T(8,128)(2,1)S(1)}, u32[]{:S(2)}, u32[]{:S(2)}) collective-permute-start(bf16[21,64,128]{2,1,0:T(8,128)(2,1)S(1)} %slice.12), channel_id=1, source_target_pairs={{0,8},{8,0},{1,9},{9,1},{2,10},{10,2},{3,11},{11,3},{4,12},{12,4},... | collective-permute-start | bytes 1032200 | tf_op jit(solution)/shard_map/ppermute | solution.py:180
  66.7 1.2 %copy-start = (bf16[26,64,128]{2,1,0:T(8,128)(2,1)}, bf16[26,64,128]{2,1,0:T(8,128)(2,1)S(1)}, u32[]{:S(2)}) copy-start(bf16[26,64,128]{2,1,0:T(8,128)(2,1)S(1)} %collective-permute-done.2.far) | copy-start | bytes 1277956
  68.0 1.0 %slice-start = ((bf16[26,64,128]{2,1,0:T(8,128)(2,1)}), bf16[21,64,128]{2,1,0:T(8,128)(2,1)S(1)}, s32[]{:S(2)}) async-start(bf16[26,64,128]{2,1,0:T(8,128)(2,1)} %copy-done), calls=%async_computation.1 | async-start | bytes 688128 | tf_op jit(solution)/shard_map/slice | solution.py:241
  68.9 9.7 %copy-start.1 = (bf16[26,64,128]{2,1,0:T(8,128)(2,1)S(1)}, bf16[26,64,128]{2,1,0:T(8,128)(2,1)}, u32[]{:S(2)}) copy-start(bf16[26,64,128]{2,1,0:T(8,128)(2,1)} %copy-done) | copy-start | bytes 1277956
  68.9 9.7 %copy-start.2 = (s32[32768]{0:T(1024)S(1)}, s32[32768]{0:T(1024)}, u32[]{:S(2)}) copy-start(s32[32768]{0:T(1024)} %param.7) | copy-start | bytes 393220
  68.9 9.7 %copy-start.3 = (s32[4,10]{1,0:T(4,128)S(1)}, s32[4,10]{1,0:T(4,128)}, u32[]{:S(2)}) copy-start(s32[4,10]{1,0:T(4,128)} %ancestors.1) | copy-start | bytes 484
  69.0 9.6 %copy-start.4 = (s32[4]{0:T(128)S(1)}, s32[4]{0:T(128)}, u32[]{:S(2)}) copy-start(s32[4]{0:T(128)} %depth.1) | copy-start | bytes 52
  69.0 9.6 %collective-permute-start.5 = (bf16[42,64,128]{2,1,0:T(8,128)(2,1)S(1)}, bf16[42,64,128]{2,1,0:T(8,128)(2,1)S(1)}, u32[]{:S(2)}, u32[]{:S(2)}) collective-permute-start(bf16[42,64,128]{2,1,0:T(8,128)(2,1)S(1)} %pad_maximum_fusion), channel_id=1, source_target_pairs={{0,8},{8,0},{1,9},{9,1},{2,10},{10,2},{3,11},{11,3},{4,12},{12,4},... | collective-permute-start | bytes 2064392 | tf_op jit(solution)/shard_map/ppermute | solution.py:180

commit v3 on v2

--- a/solution.py
+++ b/solution.py
@@ -13,9 +13,10 @@
 BLOCK = 128
 SLOTS = 10
 GROUP = 5
+DEPTHS = (7, 10)
 KEYS = (SLOTS + 1) * BLOCK
 NEG = -1e30
-VMEM_LIMIT = 24 * 1024 * 1024
+VMEM_LIMIT = 32 * 1024 * 1024
 NT = (((1,), (1,)), ((), ()))
 
 
@@ -93,77 +94,104 @@
     return (other << 8) | (order << 6) | ((source >> 6) << 3) | (source & 7)
 
 
-def picker_of(pos_row):
-    column = jnp.transpose(jnp.broadcast_to(pos_row.astype(jnp.float32), (128, 128)))
-    parts = []
-    for k in range(4):
-        lane = (lax.broadcasted_iota(jnp.int32, (128, 128), 1) + k * 128).astype(jnp.float32)
-        parts.append(jnp.where(column == lane, 1.0, 0.0).astype(jnp.bfloat16))
-    return jnp.concatenate(parts, 1)
+def picker_kernel(index, out):
+    z, in_tree = lax.axis_index("z"), lax.axis_index("x") * 2 + lax.axis_index("c")
+
+    def block(n, carry):
+        places = arrival(index[pl.ds(z * 32 + n, 1), :], in_tree).astype(jnp.float32)
+        column = jnp.transpose(jnp.broadcast_to(places, (128, 128)))
+        for k in range(4):
+            lane = (iota((128, 128), 1) + k * 128).astype(jnp.float32)
+            out[n, :, k * 128 : (k + 1) * 128] = one_hot(column == lane)
+        return carry
+
+    lax.fori_loop(0, lax.axis_index("x") * 8 + 8, block, 0)
 
 
 def attend_kernel(
-    ancestors, depth, index, keep, own, near, far, across, mate, first, rest, out,
+    ancestors, depth, pickers, keep, own, near, far, across, mate, first, rest, out,
     keys, values, local_q, kc, vc, scores, probs,
 ):
     z, in_tree = lax.axis_index("z"), lax.axis_index("x") * 2 + lax.axis_index("c")
     slabs = ((own, 0), (near, 10), (far, 0), (across, 10), (mate, 0), (first, 0), (rest, 0), (rest, 26))
     parts = ((keep, 0), (near, 31), (far, 21), (across, 0), (mate, 16), (first, 16), (rest, 16), (rest, 21))
 
-    def picked(block, raw):
-        pick = picker_of(arrival(index[pl.ds(z * 32 + block, 1), :], in_tree))
-        return jnp.dot(pick, raw, preferred_element_type=jnp.float32).astype(jnp.bfloat16)
-
-    def place_shard(j, carry):
-        raw = jnp.concatenate(
-            [jnp.concatenate([r[base + 2 * j + e] for r, base in slabs], 0) for e in range(2)], 1
+    def gathered(tiles, count):
+        return jnp.concatenate(
+            [jnp.concatenate([r[base + k] for r, base in tiles], 0) for k in range(count)], 1
         )
-        for n in range(4):
-            got = picked(j * 4 + n, raw)
-            keys[j * 4 + n] = got[:, :128]
-            values[j * 4 + n] = got[:, 128:]
+
+    def place_chip(chip, carry):
+        for core in range(2):
+            j = chip * 2 + core
+            raw = jnp.concatenate(
+                [jnp.concatenate([r[base + 2 * j + e] for r, base in slabs], 0) for e in range(2)], 1
+            )
+            pick = jnp.concatenate([pickers[j * 4 + n] for n in range(4)], 0)
+            got = jnp.dot(pick, raw, preferred_element_type=jnp.float32).astype(jnp.bfloat16)
+            for n in range(4):
+                keys[j * 4 + n] = got[n * 128 : (n + 1) * 128, :128]
+                values[j * 4 + n, :, :128] = got[n * 128 : (n + 1) * 128, 128:]
         return carry
 
-    lax.fori_loop(0, in_tree + 1, place_shard, 0)
-    raw = jnp.concatenate(
-        [jnp.concatenate([r[base + h] for r, base in parts], 0) for h in range(GROUP)], 1
-    )
+    lax.fori_loop(0, lax.axis_index("x") + 1, place_chip, 0)
+    raw = gathered(parts, GROUP)
     for n in range(4):
-        got = picked(in_tree * 4 + n, raw)
+        pick = pickers[in_tree * 4 + n]
+        got = jnp.dot(pick, raw, preferred_element_type=jnp.float32).astype(jnp.bfloat16)
         for h in range(GROUP):
             local_q[n, h * 128 : (h + 1) * 128, :] = got[:, h * 128 : (h + 1) * 128]
-    vc[:, 128:] = jnp.ones((KEYS, 128), jnp.bfloat16)
+    values[:, :, 128:] = jnp.ones((33, 128, 128), jnp.bfloat16)
+    values[32] = jnp.zeros((128, 256), jnp.bfloat16)
+    keys[32] = jnp.broadcast_to(keys[0].astype(jnp.float32)[:1], (128, 128)).astype(jnp.bfloat16)
     factor = math.log2(math.e) / math.sqrt(HEAD)
-
-    def attend(b, carry):
-        levels = depth[b]
-        for j in range(SLOTS):
-            block = ancestors[b, j] - z * 32
-            kc[j * 128 : (j + 1) * 128, :] = keys[block]
-            vc[j * 128 : (j + 1) * 128, :128] = values[block]
-        me = in_tree * 4 + b
-        kc[SLOTS * 128 :, :] = keys[me]
-        vc[SLOTS * 128 :, :128] = values[me]
-        scores[...] = lax.dot_general(local_q[b], kc[...], NT, preferred_element_type=jnp.float32)
-        slot = lax.broadcasted_iota(jnp.int32, (1, SLOTS * 128), 1) >> 7
-        bias = jnp.where(slot < levels, 0.0, NEG)
-        r = lax.broadcasted_iota(jnp.int32, (128, 128), 0)
-        n = lax.broadcasted_iota(jnp.int32, (128, 128), 1)
-        causal = jnp.where(n <= r, 0.0, NEG)
-        for h in range(GROUP):
-            rows = slice(h * 128, (h + 1) * 128)
-            s0 = scores[rows, : SLOTS * 128] + bias
-            s1 = scores[rows, SLOTS * 128 :] + causal
-            top = jnp.maximum(jnp.max(s0, 1, keepdims=True), jnp.max(s1, 1, keepdims=True))
-            probs[rows, : SLOTS * 128] = jnp.exp2((s0 - top) * factor).astype(jnp.bfloat16)
-            probs[rows, SLOTS * 128 :] = jnp.exp2((s1 - top) * factor).astype(jnp.bfloat16)
-        acc = jnp.dot(probs[...], vc[...], preferred_element_type=jnp.float32)
-        res = (acc[:, :128] / acc[:, 128:]).astype(jnp.bfloat16)
-        for h in range(GROUP):
-            out[pl.ds(pl.multiple_of(b * 128, 128), 128), h * 128 : (h + 1) * 128] = res[h * 128 : (h + 1) * 128]
-        return carry
-
-    lax.fori_loop(0, 4, attend, 0)
+    causal = jnp.where(iota((128, 128), 1) <= iota((128, 128), 0), 0.0, NEG)
+
+    def run(slots):
+        last, size = slots * 128, slots * 128 + 128
+
+        def score(b):
+            levels, me, even = depth[b], in_tree * 4 + b, b % 2
+            spare = jnp.where(levels == 0, 32, ancestors[b, 0] - z * 32)
+            for j in range(slots):
+                seen = j < levels
+                block = ancestors[b, j] - z * 32
+                kc[even, j * 128 : (j + 1) * 128, :] = keys[jnp.where(seen, block, spare)]
+                vc[even, j * 128 : (j + 1) * 128, :] = values[jnp.where(seen, block, 32)]
+            kc[even, last:size, :] = keys[me]
+            vc[even, last:size, :] = values[me]
+            scores[even, :, :size] = lax.dot_general(
+                local_q[b], kc[even, :size], NT, preferred_element_type=jnp.float32
+            )
+
+        def weigh(b):
+            even = b % 2
+            for h in range(GROUP):
+                rows = slice(h * 128, (h + 1) * 128)
+                s0 = scores[even, rows, :last]
+                s1 = scores[even, rows, last:size] + causal
+                top = jnp.maximum(jnp.max(s0, 1, keepdims=True), jnp.max(s1, 1, keepdims=True))
+                probs[even, rows, :last] = jnp.exp2((s0 - top) * factor).astype(jnp.bfloat16)
+                probs[even, rows, last:size] = jnp.exp2((s1 - top) * factor).astype(jnp.bfloat16)
+
+        def collect(b):
+            acc = jnp.dot(probs[b % 2, :, :size], vc[b % 2, :size], preferred_element_type=jnp.float32)
+            res = (acc[:, :128] / acc[:, 128:]).astype(jnp.bfloat16)
+            for h in range(GROUP):
+                out[b * 128 : (b + 1) * 128, h * 128 : (h + 1) * 128] = res[h * 128 : (h + 1) * 128]
+
+        score(0)
+        for b in range(4):
+            if b < 3:
+                score(b + 1)
+            weigh(b)
+            collect(b)
+
+    deepest = functools.reduce(jnp.maximum, [depth[b] for b in range(4)])
+    low = -1
+    for slots in DEPTHS:
+        pl.when((deepest > low) & (deepest <= slots))(functools.partial(run, slots))
+        low = slots
 
 
 SMEM = pl.BlockSpec(memory_space=pltpu.SMEM)
@@ -184,24 +212,35 @@
     return lax.all_to_all(block, axes, split_axis=0, concat_axis=0, tiled=True)
 
 
-def finish(ancestors, depth, index, *tiles):
+def pickers_of(index):
+    return pl.pallas_call(
+        picker_kernel,
+        out_shape=jax.ShapeDtypeStruct((32, 128, 512), jnp.bfloat16),
+        in_specs=[VMEM],
+        out_specs=VMEM,
+        compiler_params=pltpu.CompilerParams(vmem_limit_bytes=VMEM_LIMIT),
+        name="pickers",
+    )(index)
+
+
+def finish(ancestors, depth, pickers, *tiles):
     return pl.pallas_call(
         attend_kernel,
         out_shape=jax.ShapeDtypeStruct((512, 640), jnp.bfloat16),
         in_specs=[SMEM] * 2 + [VMEM] * 9,
         out_specs=VMEM,
         scratch_shapes=[
-            pltpu.VMEM((32, 128, 128), jnp.bfloat16),
-            pltpu.VMEM((32, 128, 128), jnp.bfloat16),
+            pltpu.VMEM((33, 128, 128), jnp.bfloat16),
+            pltpu.VMEM((33, 128, 256), jnp.bfloat16),
             pltpu.VMEM((4, 640, 128), jnp.bfloat16),
-            pltpu.VMEM((KEYS, 128), jnp.bfloat16),
-            pltpu.VMEM((KEYS, 256), jnp.bfloat16),
-            pltpu.VMEM((640, KEYS), jnp.float32),
-            pltpu.VMEM((640, KEYS), jnp.bfloat16),
+            pltpu.VMEM((2, KEYS, 128), jnp.bfloat16),
+            pltpu.VMEM((2, KEYS, 256), jnp.bfloat16),
+            pltpu.VMEM((2, 640, KEYS), jnp.float32),
+            pltpu.VMEM((2, 640, KEYS), jnp.bfloat16),
         ],
         compiler_params=pltpu.CompilerParams(vmem_limit_bytes=VMEM_LIMIT),
         name="tree_attention",
-    )(ancestors, depth, index, *tiles)
+    )(ancestors, depth, pickers, *tiles)
 
 
 def body(query_beam, key_value_beam, beam_row_index, ancestors, depth):
@@ -231,15 +270,17 @@
         compiler_params=params,
         name="regroup",
     )(landed)
+    index, ahead = lax.optimization_barrier((index, ahead))
+    pickers = pickers_of(index)
     near = ring(ahead, 1)
     far = ring(back, -1)
     mate_swapped = swap(mate)
-    near, mate_swapped = lax.optimization_barrier((near, mate_swapped))
+    near, mate_swapped, pickers = lax.optimization_barrier((near, mate_swapped, pickers))
     across = ring(near[:26], 1)
     first = swap(near[10:31])
     far, first = lax.optimization_barrier((far, first))
     rest = swap(jnp.concatenate([far[:21], across[5:]], 0))
-    return finish(ancestors, depth, index, keep, mate, near, far, across, mate_swapped, first, rest)
+    return finish(ancestors, depth, pickers, keep, mate, near, far, across, mate_swapped, first, rest)
 
 
 def solution(mesh):

time: 91.3 us -> 84.4 us (0.924)
  Pallas kernels: 15.2 us -> 10.3 us
  starting transfers between devices: 29.2 us -> 27 us
  waiting for transfers between devices: 2.99 us -> 4 us
  local copies, waits for them, and re-layouts: 1.05 us -> 0.12 us
    pallas_call x1, Pallas kernels: 12.2 us -> 6.27 us  [finish(): pl.pallas_call(attend_kernel, out_shape=jax.ShapeDtypeStruct((512, 640),...]
    ppermute x3, starting transfers between devices: 17 us -> 13.3 us  [swap(): return lax.ppermute(block, 'c', [(0, 1), (1, 0)])]
    ppermute x3, starting transfers between devices: 12.2 us -> 13.7 us  [ring(): return lax.ppermute(block, ('x', 'c'), route)]
    ppermute x3, waiting for transfers between devices: 0.01 us -> 1 us  [ring(): return lax.ppermute(block, ('x', 'c'), route)]
    pallas_call x0 -> x1, Pallas kernels: none -> 0.96 us  [pickers_of(): pl.pallas_call(picker_kernel, out_shape=jax.ShapeDtypeStruct((32, 128, 51...]
    slice x3 -> x2, local copies, waits for them, and re-layouts: 0.97 us -> 0.05 us  [body(): rest = swap(jnp.concatenate([far[:21], across[5:]], 0))]
  transfers between devices with their start and end apart: 6 -> 6, of which waited for: 2 -> 3; matrix products, arithmetic and copies ran while one was open for 0% -> 0% of each run, Pallas kernels for 0% -> 1%
where the time goes in v3:
time: 84.4 us; the launch traced here: 83.8 us
  blocking collectives  42.1 us (50%)
  starting transfers between devices  27 us (32%)
  Pallas kernels  10.3 us (12%)
  waiting for transfers between devices  4 us (5%)
    all_to_all x1, blocking collectives, exchange(): return lax.all_to_all(block, axes, split_axis=0, concat_axis=0, tiled=True)  42.1 us
    ppermute x3, starting transfers between devices, ring(): return lax.ppermute(block, ('x', 'c'), route)  13.7 us
    ppermute x3, starting transfers between devices, swap(): return lax.ppermute(block, 'c', [(0, 1), (1, 0)])  13.3 us
    pallas_call x1, Pallas kernels, finish(): pl.pallas_call(attend_kernel, out_shape=jax.ShapeDtypeStruct((512, 640),...  6.27 us
    ppermute x3, waiting for transfers between devices, swap(): return lax.ppermute(block, 'c', [(0, 1), (1, 0)])  3 us
    pallas_call x1, Pallas kernels, body(): pl.pallas_call(sort_kernel, out_shape=jax.ShapeDtypeStruct((64, 8, 896),...  2.62 us
  transfers between devices with their start and end apart: 6, of which 3 were waited for; matrix products, arithmetic and copies ran while one was open for 0% of the time, Pallas kernels for 1%

profile of v3, /device:TPU:1, one launch (start us, length us, event | category | flops | bytes accessed | tf_op | source)
XLA Modules:
  0.0 83.8 jit_solution(6098515967738483258)
XLA Ops:
  0.0 0.0 copy-start
  0.0 2.6 %sort_rows.1 = bf16[64,8,896]{2,1,0:T(8,128)(2,1)} custom-call(s32[256,128]{1,0:T(8,128)} %bitcast.1, bf16[64,5120]{1,0:T(8,128)(2,1)} %query_hbm.1, bf16[64,2048]{1,0:T(8,128)(2,1)} %pairs_hbm.1), custom_call_target="tpu_custom_call" | custom-call | tf_op jit(solution)/shard_map/sort_rows/pallas_call | solution.py:249
  2.6 42.1 %all_to_all.5.landed = bf16[64,8,896]{2,1,0:T(8,128)(2,1)S(1)} all-to-all(bf16[64,8,896]{2,1,0:T(8,128)(2,1)} %sort_rows.1), channel_id=1, replica_groups=mesh['z'=8,'x'=4,'c'=2,'t'=8] {'z','t'}, dimensions={0} | all-to-all | bytes 1835008 | tf_op jit(solution)/shard_map/all_to_all | solution.py:212
  44.8 0.4 regroup.1
  45.2 4.4 %collective-permute-start = (bf16[36,64,128]{2,1,0:T(8,128)(2,1)S(1)}, bf16[36,64,128]{2,1,0:T(8,128)(2,1)S(1)}, u32[]{:S(2)}, u32[]{:S(2)}) collective-permute-start(bf16[36,64,128]{2,1,0:T(8,128)(2,1)S(1)} %get-tuple-element.17), channel_id=1, source_target_pairs={{0,16},{8,56},{16,32},{24,8},{32,48},{40,24},{48,0},{56,40},{1,17}... | collective-permute-start | bytes 1769480 | tf_op jit(solution)/shard_map/ppermute | solution.py:204
  49.6 3.9 %collective-permute-start.1 = (bf16[21,64,128]{2,1,0:T(8,128)(2,1)S(1)}, bf16[21,64,128]{2,1,0:T(8,128)(2,1)S(1)}, u32[]{:S(2)}, u32[]{:S(2)}) collective-permute-start(bf16[21,64,128]{2,1,0:T(8,128)(2,1)S(1)} %get-tuple-element.18.own), channel_id=1, source_target_pairs={{0,8},{8,0},{1,9},{9,1},{2,10},{10,2},{3,11},{11,3},{4,12},{12,4},... | collective-permute-start | bytes 1032200 | tf_op jit(solution)/shard_map/ppermute | solution.py:208
  53.5 0.0 copy-start.1
  53.5 0.0 copy-start.2
  53.5 3.1 %collective-permute-start.2 = (bf16[26,64,128]{2,1,0:T(8,128)(2,1)S(1)}, bf16[26,64,128]{2,1,0:T(8,128)(2,1)S(1)}, u32[]{:S(2)}, u32[]{:S(2)}) collective-permute-start(bf16[26,64,128]{2,1,0:T(8,128)(2,1)S(1)} %get-tuple-element.23), channel_id=1, source_target_pairs={{0,48},{8,24},{16,0},{24,40},{32,16},{40,56},{48,32},{56,8},{1,49}... | collective-permute-start | bytes 1277960 | tf_op jit(solution)/shard_map/ppermute | solution.py:204
  56.7 0.0 copy-done
  56.7 1.0 %pickers.1 = bf16[32,128,512]{2,1,0:T(8,128)(2,1)S(1)} custom-call(s32[256,128]{1,0:T(8,128)S(1)} %bitcast.2), custom_call_target="tpu_custom_call" | custom-call | tf_op jit(solution)/shard_map/pickers/pallas_call | solution.py:216
  57.6 0.0 collective-permute-done.1.mate
  57.6 0.0 collective-permute-done.near
  57.7 6.2 %collective-permute-start.4 = (bf16[26,64,128]{2,1,0:T(8,128)(2,1)S(1)}, bf16[26,64,128]{2,1,0:T(8,128)(2,1)S(1)}, u32[]{:S(2)}, u32[]{:S(2)}) collective-permute-start(bf16[26,64,128]{2,1,0:T(8,128)(2,1)S(1)} %slice.13), channel_id=1, source_target_pairs={{0,16},{8,56},{16,32},{24,8},{32,48},{40,24},{48,0},{56,40},{1,17}... | collective-permute-start | bytes 1277960 | tf_op jit(solution)/shard_map/ppermute | solution.py:204
  64.0 2.7 %collective-permute-start.3 = (bf16[21,64,128]{2,1,0:T(8,128)(2,1)S(1)}, bf16[21,64,128]{2,1,0:T(8,128)(2,1)S(1)}, u32[]{:S(2)}, u32[]{:S(2)}) collective-permute-start(bf16[21,64,128]{2,1,0:T(8,128)(2,1)S(1)} %slice.12), channel_id=1, source_target_pairs={{0,8},{8,0},{1,9},{9,1},{2,10},{10,2},{3,11},{11,3},{4,12},{12,4},... | collective-permute-start | bytes 1032200 | tf_op jit(solution)/shard_map/ppermute | solution.py:208
  66.7 0.0 collective-permute-done.2.far
  66.7 1.2 %collective-permute-done.3.first = bf16[21,64,128]{2,1,0:T(8,128)(2,1)S(1)} collective-permute-done((bf16[21,64,128]{2,1,0:T(8,128)(2,1)S(1)}, bf16[21,64,128]{2,1,0:T(8,128)(2,1)S(1)}, u32[]{:S(2)}, u32[]{:S(2)}) %collective-permute-start.3) | collective-permute-done | bytes 344096 | tf_op jit(solution)/shard_map/ppermute | solution.py:208
  68.0 1.0 %collective-permute-done.4.across = bf16[26,64,128]{2,1,0:T(8,128)(2,1)S(1)} collective-permute-done((bf16[26,64,128]{2,1,0:T(8,128)(2,1)S(1)}, bf16[26,64,128]{2,1,0:T(8,128)(2,1)S(1)}, u32[]{:S(2)}, u32[]{:S(2)}) %collective-permute-start.4) | collective-permute-done | bytes 426016 | tf_op jit(solution)/shard_map/ppermute | solution.py:204
  69.0 0.1 pad_maximum_fusion
  69.1 6.7 %collective-permute-start.5 = (bf16[42,64,128]{2,1,0:T(8,128)(2,1)S(1)}, bf16[42,64,128]{2,1,0:T(8,128)(2,1)S(1)}, u32[]{:S(2)}, u32[]{:S(2)}) collective-permute-start(bf16[42,64,128]{2,1,0:T(8,128)(2,1)S(1)} %pad_maximum_fusion), channel_id=1, source_target_pairs={{0,8},{8,0},{1,9},{9,1},{2,10},{10,2},{3,11},{11,3},{4,12},{12,4},... | collective-permute-start | bytes 2064392 | tf_op jit(solution)/shard_map/ppermute | solution.py:208
  75.8 1.7 %collective-permute-done.5.rest = bf16[42,64,128]{2,1,0:T(8,128)(2,1)S(1)} collective-permute-done((bf16[42,64,128]{2,1,0:T(8,128)(2,1)S(1)}, bf16[42,64,128]{2,1,0:T(8,128)(2,1)S(1)}, u32[]{:S(2)}, u32[]{:S(2)}) %collective-permute-start.5) | collective-permute-done | bytes 688160 | tf_op jit(solution)/shard_map/ppermute | solution.py:208
  77.5 0.0 copy-done.1
  77.5 0.0 copy-done.2
  77.5 6.3 %tree_attention.1 = bf16[512,640]{1,0:T(8,128)(2,1)} custom-call(s32[4,10]{1,0:T(4,128)S(1)} %copy-done.1, s32[4]{0:T(128)S(1)} %copy-done.2, bf16[32,128,512]{2,1,0:T(8,128)(2,1)S(1)} %pickers.1, bf16[5,64,128]{2,1,0:T(8,128)(2,1)S(1)} %get-tuple-element.21.keep, bf16[21,64,128]{2,1,0:T(8,128)(2,1)S(1)} %get-tuple-element.18.own, ...), custom_call_target="tpu_custom_call" | custom-call | tf_op jit(solution)/shard_map/tree_attention/pallas_call | solution.py:227
  (4 shorter events, 0.1 us)
Async XLA Ops:
  0.0 56.7 %copy-start = (s32[32768]{0:T(1024)S(1)}, s32[32768]{0:T(1024)}, u32[]{:S(2)}) copy-start(s32[32768]{0:T(1024)} %param.7) | copy-start | bytes 393220
  45.2 12.4 %collective-permute-start = (bf16[36,64,128]{2,1,0:T(8,128)(2,1)S(1)}, bf16[36,64,128]{2,1,0:T(8,128)(2,1)S(1)}, u32[]{:S(2)}, u32[]{:S(2)}) collective-permute-start(bf16[36,64,128]{2,1,0:T(8,128)(2,1)S(1)} %get-tuple-element.17), channel_id=1, source_target_pairs={{0,16},{8,56},{16,32},{24,8},{32,48},{40,24},{48,0},{56,40},{1,17}... | collective-permute-start | bytes 1769480 | tf_op jit(solution)/shard_map/ppermute | solution.py:204
  49.6 8.0 %collective-permute-start.1 = (bf16[21,64,128]{2,1,0:T(8,128)(2,1)S(1)}, bf16[21,64,128]{2,1,0:T(8,128)(2,1)S(1)}, u32[]{:S(2)}, u32[]{:S(2)}) collective-permute-start(bf16[21,64,128]{2,1,0:T(8,128)(2,1)S(1)} %get-tuple-element.18.own), channel_id=1, source_target_pairs={{0,8},{8,0},{1,9},{9,1},{2,10},{10,2},{3,11},{11,3},{4,12},{12,4},... | collective-permute-start | bytes 1032200 | tf_op jit(solution)/shard_map/ppermute | solution.py:208
  53.5 24.0 %copy-start.1 = (s32[4,10]{1,0:T(4,128)S(1)}, s32[4,10]{1,0:T(4,128)}, u32[]{:S(2)}) copy-start(s32[4,10]{1,0:T(4,128)} %ancestors.1) | copy-start | bytes 484
  53.5 24.0 %copy-start.2 = (s32[4]{0:T(128)S(1)}, s32[4]{0:T(128)}, u32[]{:S(2)}) copy-start(s32[4]{0:T(128)} %depth.1) | copy-start | bytes 52
  53.5 13.2 %collective-permute-start.2 = (bf16[26,64,128]{2,1,0:T(8,128)(2,1)S(1)}, bf16[26,64,128]{2,1,0:T(8,128)(2,1)S(1)}, u32[]{:S(2)}, u32[]{:S(2)}) collective-permute-start(bf16[26,64,128]{2,1,0:T(8,128)(2,1)S(1)} %get-tuple-element.23), channel_id=1, source_target_pairs={{0,48},{8,24},{16,0},{24,40},{32,16},{40,56},{48,32},{56,8},{1,49}... | collective-permute-start | bytes 1277960 | tf_op jit(solution)/shard_map/ppermute | solution.py:204
  57.7 11.3 %collective-permute-start.4 = (bf16[26,64,128]{2,1,0:T(8,128)(2,1)S(1)}, bf16[26,64,128]{2,1,0:T(8,128)(2,1)S(1)}, u32[]{:S(2)}, u32[]{:S(2)}) collective-permute-start(bf16[26,64,128]{2,1,0:T(8,128)(2,1)S(1)} %slice.13), channel_id=1, source_target_pairs={{0,16},{8,56},{16,32},{24,8},{32,48},{40,24},{48,0},{56,40},{1,17}... | collective-permute-start | bytes 1277960 | tf_op jit(solution)/shard_map/ppermute | solution.py:204
  64.0 4.0 %collective-permute-start.3 = (bf16[21,64,128]{2,1,0:T(8,128)(2,1)S(1)}, bf16[21,64,128]{2,1,0:T(8,128)(2,1)S(1)}, u32[]{:S(2)}, u32[]{:S(2)}) collective-permute-start(bf16[21,64,128]{2,1,0:T(8,128)(2,1)S(1)} %slice.12), channel_id=1, source_target_pairs={{0,8},{8,0},{1,9},{9,1},{2,10},{10,2},{3,11},{11,3},{4,12},{12,4},... | collective-permute-start | bytes 1032200 | tf_op jit(solution)/shard_map/ppermute | solution.py:208
  69.1 8.4 %collective-permute-start.5 = (bf16[42,64,128]{2,1,0:T(8,128)(2,1)S(1)}, bf16[42,64,128]{2,1,0:T(8,128)(2,1)S(1)}, u32[]{:S(2)}, u32[]{:S(2)}) collective-permute-start(bf16[42,64,128]{2,1,0:T(8,128)(2,1)S(1)} %pad_maximum_fusion), channel_id=1, source_target_pairs={{0,8},{8,0},{1,9},{9,1},{2,10},{10,2},{3,11},{11,3},{4,12},{12,4},... | collective-permute-start | bytes 2064392 | tf_op jit(solution)/shard_map/ppermute | solution.py:208

commit v4 on v3

--- a/solution.py
+++ b/solution.py
@@ -28,7 +28,7 @@
     return lax.broadcasted_iota(jnp.int32, shape, dim)
 
 
-def sort_kernel(index_hbm, query_hbm, pairs_hbm, out, index, query, pairs, sems):
+def sort_kernel(index_hbm, query_hbm, pairs_hbm, out, index, query, pairs, made, sems, sent):
     copies = [
         pltpu.make_async_copy(src, dst, sems.at[k])
         for k, (src, dst) in enumerate(((index_hbm, index), (pairs_hbm, pairs), (query_hbm, query)))
@@ -45,12 +45,17 @@
     picker = one_hot(source.astype(jnp.int32) == iota((64, 64), 1))
     copies[1].wait()
     copies[2].wait()
+    leaving = []
     for t in range(8):
         q = jnp.dot(picker, query[:, t * 640 : (t + 1) * 640], preferred_element_type=jnp.float32)
         kv = jnp.dot(picker, pairs[:, t * 256 : (t + 1) * 256], preferred_element_type=jnp.float32)
         for z in range(8):
-            out[z * 8 + t, :, :640] = q[z * 8 : (z + 1) * 8].astype(jnp.bfloat16)
-            out[z * 8 + t, :, 640:] = kv[z * 8 : (z + 1) * 8].astype(jnp.bfloat16)
+            made[z, t, :, :640] = q[z * 8 : (z + 1) * 8].astype(jnp.bfloat16)
+            made[z, t, :, 640:] = kv[z * 8 : (z + 1) * 8].astype(jnp.bfloat16)
+        leaving.append(pltpu.make_async_copy(made.at[:, t], out.at[:, t], sent.at[t]))
+        leaving[-1].start()
+    for copy in leaving:
+        copy.wait()
 
 
 def regroup_kernel(landed, ahead, back, mate, keep, parts):
@@ -89,9 +94,9 @@
     source = idx >> 6
     behind = ((in_tree >> 1) - (source >> 4)) & 3
     behind = jnp.where((source & 8) != 0, (4 - behind) & 3, behind)
-    order = jnp.where(behind == 2, 3, jnp.where(behind == 3, 2, behind))
     other = ((source >> 3) ^ in_tree) & 1
-    return (other << 8) | (order << 6) | ((source >> 6) << 3) | (source & 7)
+    order = jnp.where(behind == 0, other * 3, jnp.where(behind == 2, 4 + other * 3, behind - (behind >> 1) + other * 4))
+    return (order << 6) | ((source >> 6) << 3) | (source & 7)
 
 
 def picker_kernel(index, out):
@@ -108,27 +113,49 @@
     lax.fori_loop(0, lax.axis_index("x") * 8 + 8, block, 0)
 
 
-def attend_kernel(
-    ancestors, depth, pickers, keep, own, near, far, across, mate, first, rest, out,
-    keys, values, local_q, kc, vc, scores, probs,
-):
-    z, in_tree = lax.axis_index("z"), lax.axis_index("x") * 2 + lax.axis_index("c")
-    slabs = ((own, 0), (near, 10), (far, 0), (across, 10), (mate, 0), (first, 0), (rest, 0), (rest, 26))
-    parts = ((keep, 0), (near, 31), (far, 21), (across, 0), (mate, 16), (first, 16), (rest, 16), (rest, 21))
-
-    def gathered(tiles, count):
-        return jnp.concatenate(
-            [jnp.concatenate([r[base + k] for r, base in tiles], 0) for k in range(count)], 1
-        )
+def gathered(tiles, count, start=0):
+    return jnp.concatenate(
+        [jnp.concatenate([r[base + start + k] for r, base in tiles], 0) for k in range(count)], 1
+    )
+
+
+def early_kernel(pickers, keep, own, near, far, mate, pairs, queries):
+    in_tree = lax.axis_index("x") * 2 + lax.axis_index("c")
+    slabs, parts = ((own, 0), (near, 10), (far, 0), (mate, 0)), ((keep, 0), (near, 31), (far, 21), (mate, 16))
 
     def place_chip(chip, carry):
         for core in range(2):
             j = chip * 2 + core
-            raw = jnp.concatenate(
-                [jnp.concatenate([r[base + 2 * j + e] for r, base in slabs], 0) for e in range(2)], 1
-            )
-            pick = jnp.concatenate([pickers[j * 4 + n] for n in range(4)], 0)
-            got = jnp.dot(pick, raw, preferred_element_type=jnp.float32).astype(jnp.bfloat16)
+            pick = jnp.concatenate([pickers[j * 4 + n, :, :256] for n in range(4)], 0)
+            got = jnp.dot(pick, gathered(slabs, 2, 2 * j), preferred_element_type=jnp.float32)
+            pairs[j] = got.astype(jnp.bfloat16)
+        return carry
+
+    lax.fori_loop(0, lax.axis_index("x") + 1, place_chip, 0)
+    pick = jnp.concatenate([pickers[in_tree * 4 + n, :, :256] for n in range(4)], 0)
+    got = jnp.dot(pick, gathered(parts, GROUP), preferred_element_type=jnp.float32)
+    queries[...] = got.astype(jnp.bfloat16)
+
+
+def attend_kernel(
+    ancestors_hbm, depth_hbm, pickers, pairs, queries, across, first, second, rest, out_hbm,
+    ancestors, depth, keys, values, local_q, kc, vc, scores, probs, out, sems, sent,
+):
+    tables = [
+        pltpu.make_async_copy(ancestors_hbm, ancestors, sems.at[0]),
+        pltpu.make_async_copy(depth_hbm, depth, sems.at[1]),
+    ]
+    for copy in tables:
+        copy.start()
+    z, in_tree = lax.axis_index("z"), lax.axis_index("x") * 2 + lax.axis_index("c")
+    slabs, parts = ((across, 10), (first, 0), (second, 0), (rest, 5)), ((across, 0), (first, 16), (second, 16), (rest, 0))
+
+    def place_chip(chip, carry):
+        for core in range(2):
+            j = chip * 2 + core
+            pick = jnp.concatenate([pickers[j * 4 + n, :, 256:] for n in range(4)], 0)
+            got = jnp.dot(pick, gathered(slabs, 2, 2 * j), preferred_element_type=jnp.float32)
+            got = (got + pairs[j].astype(jnp.float32)).astype(jnp.bfloat16)
             for n in range(4):
                 keys[j * 4 + n] = got[n * 128 : (n + 1) * 128, :128]
                 values[j * 4 + n, :, :128] = got[n * 128 : (n + 1) * 128, 128:]
@@ -137,15 +164,21 @@
     lax.fori_loop(0, lax.axis_index("x") + 1, place_chip, 0)
     raw = gathered(parts, GROUP)
     for n in range(4):
-        pick = pickers[in_tree * 4 + n]
-        got = jnp.dot(pick, raw, preferred_element_type=jnp.float32).astype(jnp.bfloat16)
+        pick = pickers[in_tree * 4 + n, :, 256:]
+        got = jnp.dot(pick, raw, preferred_element_type=jnp.float32)
+        got = (got + queries[n * 128 : (n + 1) * 128].astype(jnp.float32)).astype(jnp.bfloat16)
         for h in range(GROUP):
             local_q[n, h * 128 : (h + 1) * 128, :] = got[:, h * 128 : (h + 1) * 128]
+    for copy in tables:
+        copy.wait()
     values[:, :, 128:] = jnp.ones((33, 128, 128), jnp.bfloat16)
     values[32] = jnp.zeros((128, 256), jnp.bfloat16)
     keys[32] = jnp.broadcast_to(keys[0].astype(jnp.float32)[:1], (128, 128)).astype(jnp.bfloat16)
     factor = math.log2(math.e) / math.sqrt(HEAD)
     causal = jnp.where(iota((128, 128), 1) <= iota((128, 128), 0), 0.0, NEG)
+
+    def leaving(b):
+        return pltpu.make_async_copy(out.at[b], out_hbm.at[pl.ds(b * 128, 128)], sent.at[b])
 
     def run(slots):
         last, size = slots * 128, slots * 128 + 128
@@ -178,7 +211,8 @@
             acc = jnp.dot(probs[b % 2, :, :size], vc[b % 2, :size], preferred_element_type=jnp.float32)
             res = (acc[:, :128] / acc[:, 128:]).astype(jnp.bfloat16)
             for h in range(GROUP):
-                out[b * 128 : (b + 1) * 128, h * 128 : (h + 1) * 128] = res[h * 128 : (h + 1) * 128]
+                out[b, :, h * 128 : (h + 1) * 128] = res[h * 128 : (h + 1) * 128]
+            leaving(b).start()
 
         score(0)
         for b in range(4):
@@ -192,6 +226,8 @@
     for slots in DEPTHS:
         pl.when((deepest > low) & (deepest <= slots))(functools.partial(run, slots))
         low = slots
+    for b in range(4):
+        leaving(b).wait()
 
 
 SMEM = pl.BlockSpec(memory_space=pltpu.SMEM)
@@ -223,13 +259,29 @@
     )(index)
 
 
+def early(pickers, *tiles):
+    return pl.pallas_call(
+        early_kernel,
+        out_shape=[
+            jax.ShapeDtypeStruct((8, 512, 256), jnp.bfloat16),
+            jax.ShapeDtypeStruct((512, 640), jnp.bfloat16),
+        ],
+        in_specs=[VMEM] * 6,
+        out_specs=[VMEM] * 2,
+        compiler_params=pltpu.CompilerParams(vmem_limit_bytes=VMEM_LIMIT),
+        name="place_early",
+    )(pickers, *tiles)
+
+
 def finish(ancestors, depth, pickers, *tiles):
     return pl.pallas_call(
         attend_kernel,
         out_shape=jax.ShapeDtypeStruct((512, 640), jnp.bfloat16),
-        in_specs=[SMEM] * 2 + [VMEM] * 9,
-        out_specs=VMEM,
+        in_specs=[HBM] * 2 + [VMEM] * 7,
+        out_specs=HBM,
         scratch_shapes=[
+            pltpu.SMEM((4, SLOTS), jnp.int32),
+            pltpu.SMEM((4,), jnp.int32),
             pltpu.VMEM((33, 128, 128), jnp.bfloat16),
             pltpu.VMEM((33, 128, 256), jnp.bfloat16),
             pltpu.VMEM((4, 640, 128), jnp.bfloat16),
@@ -237,6 +289,9 @@
             pltpu.VMEM((2, KEYS, 256), jnp.bfloat16),
             pltpu.VMEM((2, 640, KEYS), jnp.float32),
             pltpu.VMEM((2, 640, KEYS), jnp.bfloat16),
+            pltpu.VMEM((4, 128, 640), jnp.bfloat16),
+            pltpu.SemaphoreType.DMA((2,)),
+            pltpu.SemaphoreType.DMA((4,)),
         ],
         compiler_params=pltpu.CompilerParams(vmem_limit_bytes=VMEM_LIMIT),
         name="tree_attention",
@@ -248,18 +303,20 @@
     bf16 = jnp.bfloat16
     packed = pl.pallas_call(
         sort_kernel,
-        out_shape=jax.ShapeDtypeStruct((64, 8, 896), bf16),
+        out_shape=jax.ShapeDtypeStruct((8, 8, 8, 896), bf16),
         in_specs=[HBM] * 3,
-        out_specs=VMEM,
+        out_specs=HBM,
         scratch_shapes=[
             pltpu.VMEM((256, 128), jnp.int32),
             pltpu.VMEM((64, 5120), bf16),
             pltpu.VMEM((64, 2048), bf16),
+            pltpu.VMEM((8, 8, 8, 896), bf16),
             pltpu.SemaphoreType.DMA((3,)),
+            pltpu.SemaphoreType.DMA((8,)),
         ],
         name="sort_rows",
     )(index, query_beam, key_value_beam)
-    landed = exchange(packed, ("z", "t"))
+    landed = exchange(packed.reshape(64, 8, 896), ("z", "t"))
     params = pltpu.CompilerParams(vmem_limit_bytes=VMEM_LIMIT)
     ahead, back, mate, keep = pl.pallas_call(
         regroup_kernel,
@@ -278,9 +335,11 @@
     near, mate_swapped, pickers = lax.optimization_barrier((near, mate_swapped, pickers))
     across = ring(near[:26], 1)
     first = swap(near[10:31])
-    far, first = lax.optimization_barrier((far, first))
-    rest = swap(jnp.concatenate([far[:21], across[5:]], 0))
-    return finish(ancestors, depth, pickers, keep, mate, near, far, across, mate_swapped, first, rest)
+    second = swap(far[:21])
+    pairs, queries = early(pickers, keep, mate, near, far, mate_swapped)
+    across, second, pairs, queries = lax.optimization_barrier((across, second, pairs, queries))
+    rest = swap(across[5:])
+    return finish(ancestors, depth, pickers, pairs, queries, across, first, second, rest)
 
 
 def solution(mesh):

time: 84.4 us -> 82.6 us (0.979)
  waiting for transfers between devices: 4 us -> 2.3 us
    ppermute x3 -> x4, waiting for transfers between devices: 3 us -> 1.25 us  [swap(): return lax.ppermute(block, 'c', [(0, 1), (1, 0)])]
    pallas_call x1, Pallas kernels: 6.27 us -> 5.15 us  [finish(): pl.pallas_call(attend_kernel, out_shape=jax.ShapeDtypeStruct((512, 640),...]
    pallas_call x1 -> x2, Pallas kernels: 2.62 us -> 3.17 us  [the longest x1 2.49 us: body(): pl.pallas_call(sort_kernel, out_shape=jax.ShapeDtypeStruct((8, 8, 8, 896)...]
    ppermute x3 -> x4, starting transfers between devices: 13.3 us -> 13.8 us  [swap(): return lax.ppermute(block, 'c', [(0, 1), (1, 0)])]
  transfers between devices with their start and end apart: 6 -> 7, of which waited for: 3 -> 2; matrix products, arithmetic and copies ran while one was open for 0% -> 0% of each run, Pallas kernels for 1% -> 2%
where the time goes in v4:
time: 82.6 us; the launch traced here: 82.2 us
  blocking collectives  42.1 us (51%)
  starting transfers between devices  27.6 us (33%)
  Pallas kernels  9.74 us (12%)
  waiting for transfers between devices  2.3 us (3%)
    all_to_all x1, blocking collectives, exchange(): return lax.all_to_all(block, axes, split_axis=0, concat_axis=0, tiled=True)  42.1 us
    ppermute x4, starting transfers between devices, swap(): return lax.ppermute(block, 'c', [(0, 1), (1, 0)])  13.8 us
    ppermute x3, starting transfers between devices, ring(): return lax.ppermute(block, ('x', 'c'), route)  13.8 us
    pallas_call x1, Pallas kernels, finish(): pl.pallas_call(attend_kernel, out_shape=jax.ShapeDtypeStruct((512, 640),...  5.15 us
    pallas_call x1, Pallas kernels, body(): pl.pallas_call(sort_kernel, out_shape=jax.ShapeDtypeStruct((8, 8, 8, 896)...  2.49 us
  transfers between devices with their start and end apart: 7, of which 2 were waited for; matrix products, arithmetic and copies ran while one was open for 0% of the time, Pallas kernels for 2%

profile of v4, /device:TPU:1, one launch (start us, length us, event | category | flops | bytes accessed | tf_op | source)
XLA Modules:
  0.0 82.2 jit_solution(6964682993546549265)
XLA Ops:
  0.0 0.0 copy-start
  0.0 2.5 %sort_rows.1 = bf16[8,8,8,896]{3,2,1,0:T(8,128)(2,1)} custom-call(s32[256,128]{1,0:T(8,128)} %bitcast.2, bf16[64,5120]{1,0:T(8,128)(2,1)} %query_hbm.1, bf16[64,2048]{1,0:T(8,128)(2,1)} %pairs_hbm.1), custom_call_target="tpu_custom_call" | custom-call | tf_op jit(solution)/shard_map/sort_rows/pallas_call | solution.py:304
  2.5 42.1 %all_to_all.5.landed = bf16[64,8,896]{2,1,0:T(8,128)(2,1)S(1)} all-to-all(bf16[64,8,896]{2,1,0:T(8,128)(2,1)} %bitcast.4), channel_id=1, replica_groups=mesh['z'=8,'x'=4,'c'=2,'t'=8] {'z','t'}, dimensions={0} | all-to-all | bytes 1835008 | tf_op jit(solution)/shard_map/all_to_all | solution.py:248
  44.7 0.4 regroup.1
  45.1 4.4 %collective-permute-start = (bf16[36,64,128]{2,1,0:T(8,128)(2,1)S(1)}, bf16[36,64,128]{2,1,0:T(8,128)(2,1)S(1)}, u32[]{:S(2)}, u32[]{:S(2)}) collective-permute-start(bf16[36,64,128]{2,1,0:T(8,128)(2,1)S(1)} %get-tuple-element.21), channel_id=1, source_target_pairs={{0,16},{8,56},{16,32},{24,8},{32,48},{40,24},{48,0},{56,40},{1,17}... | collective-permute-start | bytes 1769480 | tf_op jit(solution)/shard_map/ppermute | solution.py:240
  49.5 3.9 %collective-permute-start.1 = (bf16[21,64,128]{2,1,0:T(8,128)(2,1)S(1)}, bf16[21,64,128]{2,1,0:T(8,128)(2,1)S(1)}, u32[]{:S(2)}, u32[]{:S(2)}) collective-permute-start(bf16[21,64,128]{2,1,0:T(8,128)(2,1)S(1)} %get-tuple-element.22.own), channel_id=1, source_target_pairs={{0,8},{8,0},{1,9},{9,1},{2,10},{10,2},{3,11},{11,3},{4,12},{12,4},... | collective-permute-start | bytes 1032200 | tf_op jit(solution)/shard_map/ppermute | solution.py:244
  53.4 3.1 %collective-permute-start.3 = (bf16[26,64,128]{2,1,0:T(8,128)(2,1)S(1)}, bf16[26,64,128]{2,1,0:T(8,128)(2,1)S(1)}, u32[]{:S(2)}, u32[]{:S(2)}) collective-permute-start(bf16[26,64,128]{2,1,0:T(8,128)(2,1)S(1)} %get-tuple-element.26), channel_id=1, source_target_pairs={{0,48},{8,24},{16,0},{24,40},{32,16},{40,56},{48,32},{56,8},{1,49}... | collective-permute-start | bytes 1277960 | tf_op jit(solution)/shard_map/ppermute | solution.py:240
  56.5 0.0 copy-done
  56.5 1.0 %pickers.1 = bf16[32,128,512]{2,1,0:T(8,128)(2,1)S(1)} custom-call(s32[256,128]{1,0:T(8,128)S(1)} %bitcast.3), custom_call_target="tpu_custom_call" | custom-call | tf_op jit(solution)/shard_map/pickers/pallas_call | solution.py:252
  57.5 0.0 collective-permute-done.1.mate
  57.5 0.0 collective-permute-done.near
  57.6 0.0 copy-start.1
  57.6 0.0 copy-start.2
  57.6 6.3 %collective-permute-start.2 = (bf16[26,64,128]{2,1,0:T(8,128)(2,1)S(1)}, bf16[26,64,128]{2,1,0:T(8,128)(2,1)S(1)}, u32[]{:S(2)}, u32[]{:S(2)}) collective-permute-start(bf16[26,64,128]{2,1,0:T(8,128)(2,1)S(1)} %slice.12), channel_id=1, source_target_pairs={{0,16},{8,56},{16,32},{24,8},{32,48},{40,24},{48,0},{56,40},{1,17}... | collective-permute-start | bytes 1277960 | tf_op jit(solution)/shard_map/ppermute | solution.py:240
  63.9 1.0 %collective-permute-done.3.far = bf16[26,64,128]{2,1,0:T(8,128)(2,1)S(1)} collective-permute-done((bf16[26,64,128]{2,1,0:T(8,128)(2,1)S(1)}, bf16[26,64,128]{2,1,0:T(8,128)(2,1)S(1)}, u32[]{:S(2)}, u32[]{:S(2)}) %collective-permute-start.3) | collective-permute-done | bytes 426016 | tf_op jit(solution)/shard_map/ppermute | solution.py:240
  64.9 1.9 %collective-permute-start.4 = (bf16[21,64,128]{2,1,0:T(8,128)(2,1)S(1)}, bf16[21,64,128]{2,1,0:T(8,128)(2,1)S(1)}, u32[]{:S(2)}, u32[]{:S(2)}) collective-permute-start(bf16[21,64,128]{2,1,0:T(8,128)(2,1)S(1)} %slice.16), channel_id=1, source_target_pairs={{0,8},{8,0},{1,9},{9,1},{2,10},{10,2},{3,11},{11,3},{4,12},{12,4},... | collective-permute-start | bytes 1032200 | tf_op jit(solution)/shard_map/ppermute | solution.py:244
  66.9 2.4 %collective-permute-start.5 = (bf16[21,64,128]{2,1,0:T(8,128)(2,1)S(1)}, bf16[21,64,128]{2,1,0:T(8,128)(2,1)S(1)}, u32[]{:S(2)}, u32[]{:S(2)}) collective-permute-start(bf16[21,64,128]{2,1,0:T(8,128)(2,1)S(1)} %slice.14), channel_id=1, source_target_pairs={{0,8},{8,0},{1,9},{9,1},{2,10},{10,2},{3,11},{11,3},{4,12},{12,4},... | collective-permute-start | bytes 1032200 | tf_op jit(solution)/shard_map/ppermute | solution.py:244
  69.3 0.7 place_early.1
  70.0 0.0 collective-permute-done.4.second
  70.0 0.0 collective-permute-done.2.across
  70.0 5.6 %collective-permute-start.6 = (bf16[21,64,128]{2,1,0:T(8,128)(2,1)S(1)}, bf16[21,64,128]{2,1,0:T(8,128)(2,1)S(1)}, u32[]{:S(2)}, u32[]{:S(2)}) collective-permute-start(bf16[21,64,128]{2,1,0:T(8,128)(2,1)S(1)} %slice.15), channel_id=1, source_target_pairs={{0,8},{8,0},{1,9},{9,1},{2,10},{10,2},{3,11},{11,3},{4,12},{12,4},... | collective-permute-start | bytes 1032200 | tf_op jit(solution)/shard_map/ppermute | solution.py:244
  75.6 0.0 collective-permute-done.5.first
  75.6 1.2 %collective-permute-done.6.rest = bf16[21,64,128]{2,1,0:T(8,128)(2,1)S(1)} collective-permute-done((bf16[21,64,128]{2,1,0:T(8,128)(2,1)S(1)}, bf16[21,64,128]{2,1,0:T(8,128)(2,1)S(1)}, u32[]{:S(2)}, u32[]{:S(2)}) %collective-permute-start.6) | collective-permute-done | bytes 344096 | tf_op jit(solution)/shard_map/ppermute | solution.py:244
  76.9 0.0 copy-done.1
  76.9 0.0 copy-done.2
  76.9 5.2 %tree_attention.1 = bf16[512,640]{1,0:T(8,128)(2,1)} custom-call(s32[4,10]{1,0:T(4,128)S(1)} %copy-done.1, s32[4]{0:T(128)S(1)} %copy-done.2, bf16[32,128,512]{2,1,0:T(8,128)(2,1)S(1)} %pickers.1, bf16[8,512,256]{2,1,0:T(8,128)(2,1)S(1)} %get-tuple-element.31.pairs, bf16[512,640]{1,0:T(8,128)(2,1)S(1)} %get-tuple-element.32.queries, ...), custom_call_target="tpu_custom_call" | custom-call | tf_op jit(solution)/shard_map/tree_attention/pallas_call | solution.py:277
  (4 shorter events, 0.1 us)
Async XLA Ops:
  0.0 56.5 %copy-start = (s32[32768]{0:T(1024)S(1)}, s32[32768]{0:T(1024)}, u32[]{:S(2)}) copy-start(s32[32768]{0:T(1024)} %param.7) | copy-start | bytes 393220
  45.1 12.4 %collective-permute-start = (bf16[36,64,128]{2,1,0:T(8,128)(2,1)S(1)}, bf16[36,64,128]{2,1,0:T(8,128)(2,1)S(1)}, u32[]{:S(2)}, u32[]{:S(2)}) collective-permute-start(bf16[36,64,128]{2,1,0:T(8,128)(2,1)S(1)} %get-tuple-element.21), channel_id=1, source_target_pairs={{0,16},{8,56},{16,32},{24,8},{32,48},{40,24},{48,0},{56,40},{1,17}... | collective-permute-start | bytes 1769480 | tf_op jit(solution)/shard_map/ppermute | solution.py:240
  49.5 8.0 %collective-permute-start.1 = (bf16[21,64,128]{2,1,0:T(8,128)(2,1)S(1)}, bf16[21,64,128]{2,1,0:T(8,128)(2,1)S(1)}, u32[]{:S(2)}, u32[]{:S(2)}) collective-permute-start(bf16[21,64,128]{2,1,0:T(8,128)(2,1)S(1)} %get-tuple-element.22.own), channel_id=1, source_target_pairs={{0,8},{8,0},{1,9},{9,1},{2,10},{10,2},{3,11},{11,3},{4,12},{12,4},... | collective-permute-start | bytes 1032200 | tf_op jit(solution)/shard_map/ppermute | solution.py:244
  53.4 11.5 %collective-permute-start.3 = (bf16[26,64,128]{2,1,0:T(8,128)(2,1)S(1)}, bf16[26,64,128]{2,1,0:T(8,128)(2,1)S(1)}, u32[]{:S(2)}, u32[]{:S(2)}) collective-permute-start(bf16[26,64,128]{2,1,0:T(8,128)(2,1)S(1)} %get-tuple-element.26), channel_id=1, source_target_pairs={{0,48},{8,24},{16,0},{24,40},{32,16},{40,56},{48,32},{56,8},{1,49}... | collective-permute-start | bytes 1277960 | tf_op jit(solution)/shard_map/ppermute | solution.py:240
  57.6 19.3 %copy-start.1 = (s32[4,10]{1,0:T(4,128)S(1)}, s32[4,10]{1,0:T(4,128)}, u32[]{:S(2)}) copy-start(s32[4,10]{1,0:T(4,128)} %ancestors_hbm.1) | copy-start | bytes 484
  57.6 19.3 %copy-start.2 = (s32[4]{0:T(128)S(1)}, s32[4]{0:T(128)}, u32[]{:S(2)}) copy-start(s32[4]{0:T(128)} %depth_hbm.1) | copy-start | bytes 52
  57.6 12.4 %collective-permute-start.2 = (bf16[26,64,128]{2,1,0:T(8,128)(2,1)S(1)}, bf16[26,64,128]{2,1,0:T(8,128)(2,1)S(1)}, u32[]{:S(2)}, u32[]{:S(2)}) collective-permute-start(bf16[26,64,128]{2,1,0:T(8,128)(2,1)S(1)} %slice.12), channel_id=1, source_target_pairs={{0,16},{8,56},{16,32},{24,8},{32,48},{40,24},{48,0},{56,40},{1,17}... | collective-permute-start | bytes 1277960 | tf_op jit(solution)/shard_map/ppermute | solution.py:240
  64.9 5.1 %collective-permute-start.4 = (bf16[21,64,128]{2,1,0:T(8,128)(2,1)S(1)}, bf16[21,64,128]{2,1,0:T(8,128)(2,1)S(1)}, u32[]{:S(2)}, u32[]{:S(2)}) collective-permute-start(bf16[21,64,128]{2,1,0:T(8,128)(2,1)S(1)} %slice.16), channel_id=1, source_target_pairs={{0,8},{8,0},{1,9},{9,1},{2,10},{10,2},{3,11},{11,3},{4,12},{12,4},... | collective-permute-start | bytes 1032200 | tf_op jit(solution)/shard_map/ppermute | solution.py:244
  66.9 8.7 %collective-permute-start.5 = (bf16[21,64,128]{2,1,0:T(8,128)(2,1)S(1)}, bf16[21,64,128]{2,1,0:T(8,128)(2,1)S(1)}, u32[]{:S(2)}, u32[]{:S(2)}) collective-permute-start(bf16[21,64,128]{2,1,0:T(8,128)(2,1)S(1)} %slice.14), channel_id=1, source_target_pairs={{0,8},{8,0},{1,9},{9,1},{2,10},{10,2},{3,11},{11,3},{4,12},{12,4},... | collective-permute-start | bytes 1032200 | tf_op jit(solution)/shard_map/ppermute | solution.py:244
  70.0 6.8 %collective-permute-start.6 = (bf16[21,64,128]{2,1,0:T(8,128)(2,1)S(1)}, bf16[21,64,128]{2,1,0:T(8,128)(2,1)S(1)}, u32[]{:S(2)}, u32[]{:S(2)}) collective-permute-start(bf16[21,64,128]{2,1,0:T(8,128)(2,1)S(1)} %slice.15), channel_id=1, source_target_pairs={{0,8},{8,0},{1,9},{9,1},{2,10},{10,2},{3,11},{11,3},{4,12},{12,4},... | collective-permute-start | bytes 1032200 | tf_op jit(solution)/shard_map/ppermute | solution.py:244

commit v5 on v4

--- a/solution.py
+++ b/solution.py
@@ -58,7 +58,7 @@
         copy.wait()
 
 
-def regroup_kernel(landed, ahead, back, mate, keep, parts):
+def regroup_kernel(landed, ahead, back, late, mate, keep, parts):
     x, c = lax.axis_index("x"), lax.axis_index("c")
     want, have = iota((128, 128), 0), iota((128, 128), 1)
     turn = one_hot(((want >> 4) == (have & 7)) & ((want & 15) == (have >> 3)))
@@ -82,8 +82,8 @@
 
     ahead[0:5] = part(2, 0)
     ahead[5:10] = part(2, 1)
-    ahead[26:31] = part(way, 1)
-    ahead[31:36] = part(way, 0)
+    late[0:5] = part(way, 1)
+    late[5:10] = part(way, 0)
     back[16:21] = part(-way, 1)
     back[21:26] = part(-way, 0)
     mate[16:21] = part(0, 1)
@@ -100,17 +100,19 @@
 
 
 def picker_kernel(index, out):
-    z, in_tree = lax.axis_index("z"), lax.axis_index("x") * 2 + lax.axis_index("c")
-
-    def block(n, carry):
-        places = arrival(index[pl.ds(z * 32 + n, 1), :], in_tree).astype(jnp.float32)
-        column = jnp.transpose(jnp.broadcast_to(places, (128, 128)))
-        for k in range(4):
-            lane = (iota((128, 128), 1) + k * 128).astype(jnp.float32)
-            out[n, :, k * 128 : (k + 1) * 128] = one_hot(column == lane)
-        return carry
-
-    lax.fori_loop(0, lax.axis_index("x") * 8 + 8, block, 0)
+    z, x, c = (lax.axis_index(n) for n in ("z", "x", "c"))
+    places = arrival(index[pl.ds(z * 32, 32), :], x * 2 + c).astype(jnp.float32)
+    columns = jnp.transpose(jnp.concatenate([places, jnp.zeros((96, 128), jnp.float32)], 0))
+    lanes = [(iota((128, 128), 1) + k * 128).astype(jnp.float32) for k in range(4)]
+
+    def chip_blocks(chip):
+        for n in range(chip * 8, chip * 8 + 8):
+            column = jnp.broadcast_to(columns[:, n : n + 1], (128, 128))
+            for k in range(4):
+                out[n, :, k * 128 : (k + 1) * 128] = one_hot(column == lanes[k])
+
+    for chip in range(4):
+        pl.when(chip <= x)(functools.partial(chip_blocks, chip))
 
 
 def gathered(tiles, count, start=0):
@@ -119,9 +121,8 @@
     )
 
 
-def early_kernel(pickers, keep, own, near, far, mate, pairs, queries):
-    in_tree = lax.axis_index("x") * 2 + lax.axis_index("c")
-    slabs, parts = ((own, 0), (near, 10), (far, 0), (mate, 0)), ((keep, 0), (near, 31), (far, 21), (mate, 16))
+def early_kernel(pickers, own, near, far, mate, pairs):
+    slabs = ((own, 0), (near, 10), (far, 0), (mate, 0))
 
     def place_chip(chip, carry):
         for core in range(2):
@@ -132,13 +133,10 @@
         return carry
 
     lax.fori_loop(0, lax.axis_index("x") + 1, place_chip, 0)
-    pick = jnp.concatenate([pickers[in_tree * 4 + n, :, :256] for n in range(4)], 0)
-    got = jnp.dot(pick, gathered(parts, GROUP), preferred_element_type=jnp.float32)
-    queries[...] = got.astype(jnp.bfloat16)
 
 
 def attend_kernel(
-    ancestors_hbm, depth_hbm, pickers, pairs, queries, across, first, second, rest, out_hbm,
+    ancestors_hbm, depth_hbm, pickers, pairs, keep, far, mate, across, first, second, rest, out_hbm,
     ancestors, depth, keys, values, local_q, kc, vc, scores, probs, out, sems, sent,
 ):
     tables = [
@@ -148,7 +146,8 @@
     for copy in tables:
         copy.start()
     z, in_tree = lax.axis_index("z"), lax.axis_index("x") * 2 + lax.axis_index("c")
-    slabs, parts = ((across, 10), (first, 0), (second, 0), (rest, 5)), ((across, 0), (first, 16), (second, 16), (rest, 0))
+    slabs = ((across, 10), (first, 0), (second, 0), (rest, 5))
+    parts = ((keep, 0), (across, 31), (far, 21), (mate, 16), (across, 0), (rest, 21), (second, 16), (rest, 0))
 
     def place_chip(chip, carry):
         for core in range(2):
@@ -164,9 +163,7 @@
     lax.fori_loop(0, lax.axis_index("x") + 1, place_chip, 0)
     raw = gathered(parts, GROUP)
     for n in range(4):
-        pick = pickers[in_tree * 4 + n, :, 256:]
-        got = jnp.dot(pick, raw, preferred_element_type=jnp.float32)
-        got = (got + queries[n * 128 : (n + 1) * 128].astype(jnp.float32)).astype(jnp.bfloat16)
+        got = jnp.dot(pickers[in_tree * 4 + n], raw, preferred_element_type=jnp.float32).astype(jnp.bfloat16)
         for h in range(GROUP):
             local_q[n, h * 128 : (h + 1) * 128, :] = got[:, h * 128 : (h + 1) * 128]
     for copy in tables:
@@ -262,12 +259,9 @@
 def early(pickers, *tiles):
     return pl.pallas_call(
         early_kernel,
-        out_shape=[
-            jax.ShapeDtypeStruct((8, 512, 256), jnp.bfloat16),
-            jax.ShapeDtypeStruct((512, 640), jnp.bfloat16),
-        ],
-        in_specs=[VMEM] * 6,
-        out_specs=[VMEM] * 2,
+        out_shape=jax.ShapeDtypeStruct((8, 512, 256), jnp.bfloat16),
+        in_specs=[VMEM] * 5,
+        out_specs=VMEM,
         compiler_params=pltpu.CompilerParams(vmem_limit_bytes=VMEM_LIMIT),
         name="place_early",
     )(pickers, *tiles)
@@ -277,7 +271,7 @@
     return pl.pallas_call(
         attend_kernel,
         out_shape=jax.ShapeDtypeStruct((512, 640), jnp.bfloat16),
-        in_specs=[HBM] * 2 + [VMEM] * 7,
+        in_specs=[HBM] * 2 + [VMEM] * 9,
         out_specs=HBM,
         scratch_shapes=[
             pltpu.SMEM((4, SLOTS), jnp.int32),
@@ -318,11 +312,11 @@
     )(index, query_beam, key_value_beam)
     landed = exchange(packed.reshape(64, 8, 896), ("z", "t"))
     params = pltpu.CompilerParams(vmem_limit_bytes=VMEM_LIMIT)
-    ahead, back, mate, keep = pl.pallas_call(
+    ahead, back, late, mate, keep = pl.pallas_call(
         regroup_kernel,
-        out_shape=[jax.ShapeDtypeStruct((n, 64, 128), bf16) for n in (36, 26, 21, 5)],
+        out_shape=[jax.ShapeDtypeStruct((n, 64, 128), bf16) for n in (26, 26, 10, 21, 5)],
         in_specs=[VMEM],
-        out_specs=[VMEM] * 4,
+        out_specs=[VMEM] * 5,
         scratch_shapes=[pltpu.VMEM((8, GROUP, 64, 128), bf16)],
         compiler_params=params,
         name="regroup",
@@ -331,15 +325,16 @@
     pickers = pickers_of(index)
     near = ring(ahead, 1)
     far = ring(back, -1)
-    mate_swapped = swap(mate)
-    near, mate_swapped, pickers = lax.optimization_barrier((near, mate_swapped, pickers))
-    across = ring(near[:26], 1)
-    first = swap(near[10:31])
+    own, mate = mate, swap(mate)
+    near, mate = lax.optimization_barrier((near, mate))
+    across = ring(jnp.concatenate([near, late], 0), 1)
+    first = swap(near[10:])
+    far, pickers = lax.optimization_barrier((far, pickers))
     second = swap(far[:21])
-    pairs, queries = early(pickers, keep, mate, near, far, mate_swapped)
-    across, second, pairs, queries = lax.optimization_barrier((across, second, pairs, queries))
-    rest = swap(across[5:])
-    return finish(ancestors, depth, pickers, pairs, queries, across, first, second, rest)
+    pairs = early(pickers, own, near, far, mate)
+    across, first, second, pairs = lax.optimization_barrier((across, first, second, pairs))
+    rest = swap(across[5:31])
+    return finish(ancestors, depth, pickers, pairs, keep, far, mate, across, first, second, rest)
 
 
 def solution(mesh):

time: 82.6 us -> 81.6 us (0.988)
  starting transfers between devices: 27.6 us -> 23.9 us
  waiting for transfers between devices: 2.3 us -> 5.66 us
    ppermute x3, starting transfers between devices: 13.8 us -> 10.9 us  [ring(): return lax.ppermute(block, ('x', 'c'), route)]
    ppermute x3, waiting for transfers between devices: 1.05 us -> 3.09 us  [ring(): return lax.ppermute(block, ('x', 'c'), route)]
    ppermute x4, waiting for transfers between devices: 1.25 us -> 2.57 us  [swap(): return lax.ppermute(block, 'c', [(0, 1), (1, 0)])]
  transfers between devices with their start and end apart: 7 -> 7, of which waited for: 2 -> 3; matrix products, arithmetic and copies ran while one was open for 0% -> 0% of each run, Pallas kernels for 2% -> 1%
where the time goes in v5:
time: 81.6 us; the launch traced here: 81.2 us
  blocking collectives  42.1 us (52%)
  starting transfers between devices  23.9 us (29%)
  Pallas kernels  8.98 us (11%)
  waiting for transfers between devices  5.66 us (7%)
    all_to_all x1, blocking collectives, exchange(): return lax.all_to_all(block, axes, split_axis=0, concat_axis=0, tiled=True)  42.1 us
    ppermute x4, starting transfers between devices, swap(): return lax.ppermute(block, 'c', [(0, 1), (1, 0)])  13 us
    ppermute x3, starting transfers between devices, ring(): return lax.ppermute(block, ('x', 'c'), route)  10.9 us
    pallas_call x1, Pallas kernels, finish(): pl.pallas_call(attend_kernel, out_shape=jax.ShapeDtypeStruct((512, 640),...  5.34 us
    ppermute x3, waiting for transfers between devices, ring(): return lax.ppermute(block, ('x', 'c'), route)  3.09 us
    ppermute x4, waiting for transfers between devices, swap(): return lax.ppermute(block, 'c', [(0, 1), (1, 0)])  2.57 us
    pallas_call x1, Pallas kernels, body(): pl.pallas_call(sort_kernel, out_shape=jax.ShapeDtypeStruct((8, 8, 8, 896)...  2.48 us
  transfers between devices with their start and end apart: 7, of which 3 were waited for; matrix products, arithmetic and copies ran while one was open for 0% of the time, Pallas kernels for 1%

profile of v5, /device:TPU:1, one launch (start us, length us, event | category | flops | bytes accessed | tf_op | source)
XLA Modules:
  0.0 81.2 jit_solution(7954673687046947965)
XLA Ops:
  0.0 0.0 copy-start
  0.0 2.5 %sort_rows.1 = bf16[8,8,8,896]{3,2,1,0:T(8,128)(2,1)} custom-call(s32[256,128]{1,0:T(8,128)} %bitcast.2, bf16[64,5120]{1,0:T(8,128)(2,1)} %query_hbm.1, bf16[64,2048]{1,0:T(8,128)(2,1)} %pairs_hbm.1), custom_call_target="tpu_custom_call" | custom-call | tf_op jit(solution)/shard_map/sort_rows/pallas_call | solution.py:298
  2.5 42.1 %all_to_all.5.landed = bf16[64,8,896]{2,1,0:T(8,128)(2,1)S(1)} all-to-all(bf16[64,8,896]{2,1,0:T(8,128)(2,1)} %bitcast.4), channel_id=1, replica_groups=mesh['z'=8,'x'=4,'c'=2,'t'=8] {'z','t'}, dimensions={0} | all-to-all | bytes 1835008 | tf_op jit(solution)/shard_map/all_to_all | solution.py:245
  44.6 0.5 regroup.1
  45.1 4.4 %collective-permute-start.1 = (bf16[26,64,128]{2,1,0:T(8,128)(2,1)S(1)}, bf16[26,64,128]{2,1,0:T(8,128)(2,1)S(1)}, u32[]{:S(2)}, u32[]{:S(2)}) collective-permute-start(bf16[26,64,128]{2,1,0:T(8,128)(2,1)S(1)} %get-tuple-element.24), channel_id=1, source_target_pairs={{0,16},{8,56},{16,32},{24,8},{32,48},{40,24},{48,0},{56,40},{1,17}... | collective-permute-start | bytes 1277960 | tf_op jit(solution)/shard_map/ppermute | solution.py:237
  49.5 3.9 %collective-permute-start.2 = (bf16[21,64,128]{2,1,0:T(8,128)(2,1)S(1)}, bf16[21,64,128]{2,1,0:T(8,128)(2,1)S(1)}, u32[]{:S(2)}, u32[]{:S(2)}) collective-permute-start(bf16[21,64,128]{2,1,0:T(8,128)(2,1)S(1)} %get-tuple-element.25.own), channel_id=1, source_target_pairs={{0,8},{8,0},{1,9},{9,1},{2,10},{10,2},{3,11},{11,3},{4,12},{12,4},... | collective-permute-start | bytes 1032200 | tf_op jit(solution)/shard_map/ppermute | solution.py:241
  53.4 3.1 %collective-permute-start = (bf16[26,64,128]{2,1,0:T(8,128)(2,1)S(1)}, bf16[26,64,128]{2,1,0:T(8,128)(2,1)S(1)}, u32[]{:S(2)}, u32[]{:S(2)}) collective-permute-start(bf16[26,64,128]{2,1,0:T(8,128)(2,1)S(1)} %get-tuple-element.20), channel_id=1, source_target_pairs={{0,48},{8,24},{16,0},{24,40},{32,16},{40,56},{48,32},{56,8},{1,49}... | collective-permute-start | bytes 1277960 | tf_op jit(solution)/shard_map/ppermute | solution.py:237
  56.5 0.0 collective-permute-done.2.mate
  56.5 0.0 collective-permute-done.1.near
  56.5 0.1 pad_maximum_fusion
  56.6 3.4 %collective-permute-start.3 = (bf16[36,64,128]{2,1,0:T(8,128)(2,1)S(1)}, bf16[36,64,128]{2,1,0:T(8,128)(2,1)S(1)}, u32[]{:S(2)}, u32[]{:S(2)}) collective-permute-start(bf16[36,64,128]{2,1,0:T(8,128)(2,1)S(1)} %pad_maximum_fusion), channel_id=1, source_target_pairs={{0,16},{8,56},{16,32},{24,8},{32,48},{40,24},{48,0},{56,40},{1,17}... | collective-permute-start | bytes 1769480 | tf_op jit(solution)/shard_map/ppermute | solution.py:237
  60.0 0.0 copy-done
  60.0 0.4 pickers.1
  60.4 3.1 %collective-permute-done.far = bf16[26,64,128]{2,1,0:T(8,128)(2,1)S(1)} collective-permute-done((bf16[26,64,128]{2,1,0:T(8,128)(2,1)S(1)}, bf16[26,64,128]{2,1,0:T(8,128)(2,1)S(1)}, u32[]{:S(2)}, u32[]{:S(2)}) %collective-permute-start) | collective-permute-done | bytes 426016 | tf_op jit(solution)/shard_map/ppermute | solution.py:237
  63.5 3.6 %collective-permute-start.5 = (bf16[21,64,128]{2,1,0:T(8,128)(2,1)S(1)}, bf16[21,64,128]{2,1,0:T(8,128)(2,1)S(1)}, u32[]{:S(2)}, u32[]{:S(2)}) collective-permute-start(bf16[21,64,128]{2,1,0:T(8,128)(2,1)S(1)} %slice.10), channel_id=1, source_target_pairs={{0,8},{8,0},{1,9},{9,1},{2,10},{10,2},{3,11},{11,3},{4,12},{12,4},... | collective-permute-start | bytes 1032200 | tf_op jit(solution)/shard_map/ppermute | solution.py:241
  67.1 0.0 copy-start.1
  67.2 0.0 copy-start.2
  67.2 1.9 %collective-permute-start.4 = (bf16[16,64,128]{2,1,0:T(8,128)(2,1)S(1)}, bf16[16,64,128]{2,1,0:T(8,128)(2,1)S(1)}, u32[]{:S(2)}, u32[]{:S(2)}) collective-permute-start(bf16[16,64,128]{2,1,0:T(8,128)(2,1)S(1)} %slice.9), channel_id=1, source_target_pairs={{0,8},{8,0},{1,9},{9,1},{2,10},{10,2},{3,11},{11,3},{4,12},{12,4},... | collective-permute-start | bytes 786440 | tf_op jit(solution)/shard_map/ppermute | solution.py:241
  69.1 0.3 place_early.1.pairs
  69.4 1.2 %collective-permute-done.4.first = bf16[16,64,128]{2,1,0:T(8,128)(2,1)S(1)} collective-permute-done((bf16[16,64,128]{2,1,0:T(8,128)(2,1)S(1)}, bf16[16,64,128]{2,1,0:T(8,128)(2,1)S(1)}, u32[]{:S(2)}, u32[]{:S(2)}) %collective-permute-start.4) | collective-permute-done | bytes 262176 | tf_op jit(solution)/shard_map/ppermute | solution.py:241
  70.6 0.0 collective-permute-done.5.second
  70.6 0.0 collective-permute-done.3.across
  70.6 3.6 %collective-permute-start.6 = (bf16[26,64,128]{2,1,0:T(8,128)(2,1)S(1)}, bf16[26,64,128]{2,1,0:T(8,128)(2,1)S(1)}, u32[]{:S(2)}, u32[]{:S(2)}) collective-permute-start(bf16[26,64,128]{2,1,0:T(8,128)(2,1)S(1)} %slice.11), channel_id=1, source_target_pairs={{0,8},{8,0},{1,9},{9,1},{2,10},{10,2},{3,11},{11,3},{4,12},{12,4},... | collective-permute-start | bytes 1277960 | tf_op jit(solution)/shard_map/ppermute | solution.py:241
  74.3 1.4 %collective-permute-done.6.rest = bf16[26,64,128]{2,1,0:T(8,128)(2,1)S(1)} collective-permute-done((bf16[26,64,128]{2,1,0:T(8,128)(2,1)S(1)}, bf16[26,64,128]{2,1,0:T(8,128)(2,1)S(1)}, u32[]{:S(2)}, u32[]{:S(2)}) %collective-permute-start.6) | collective-permute-done | bytes 426016 | tf_op jit(solution)/shard_map/ppermute | solution.py:241
  75.6 0.0 copy-done.1
  75.7 0.0 copy-done.2
  75.7 5.3 %tree_attention.1 = bf16[512,640]{1,0:T(8,128)(2,1)} custom-call(s32[4,10]{1,0:T(4,128)S(1)} %copy-done.1, s32[4]{0:T(128)S(1)} %copy-done.2, bf16[32,128,512]{2,1,0:T(8,128)(2,1)S(1)} %pickers.1, bf16[8,512,256]{2,1,0:T(8,128)(2,1)S(1)} %place_early.1.pairs, bf16[5,64,128]{2,1,0:T(8,128)(2,1)S(1)} %get-tuple-element.31.keep, ...), custom_call_target="tpu_custom_call" | custom-call | tf_op jit(solution)/shard_map/tree_attention/pallas_call | solution.py:271
  (3 shorter events, 0.1 us)
Async XLA Ops:
  0.0 60.0 %copy-start = (s32[32768]{0:T(1024)S(1)}, s32[32768]{0:T(1024)}, u32[]{:S(2)}) copy-start(s32[32768]{0:T(1024)} %param.7) | copy-start | bytes 393220
  45.1 11.4 %collective-permute-start.1 = (bf16[26,64,128]{2,1,0:T(8,128)(2,1)S(1)}, bf16[26,64,128]{2,1,0:T(8,128)(2,1)S(1)}, u32[]{:S(2)}, u32[]{:S(2)}) collective-permute-start(bf16[26,64,128]{2,1,0:T(8,128)(2,1)S(1)} %get-tuple-element.24), channel_id=1, source_target_pairs={{0,16},{8,56},{16,32},{24,8},{32,48},{40,24},{48,0},{56,40},{1,17}... | collective-permute-start | bytes 1277960 | tf_op jit(solution)/shard_map/ppermute | solution.py:237
  49.5 7.0 %collective-permute-start.2 = (bf16[21,64,128]{2,1,0:T(8,128)(2,1)S(1)}, bf16[21,64,128]{2,1,0:T(8,128)(2,1)S(1)}, u32[]{:S(2)}, u32[]{:S(2)}) collective-permute-start(bf16[21,64,128]{2,1,0:T(8,128)(2,1)S(1)} %get-tuple-element.25.own), channel_id=1, source_target_pairs={{0,8},{8,0},{1,9},{9,1},{2,10},{10,2},{3,11},{11,3},{4,12},{12,4},... | collective-permute-start | bytes 1032200 | tf_op jit(solution)/shard_map/ppermute | solution.py:241
  53.4 10.1 %collective-permute-start = (bf16[26,64,128]{2,1,0:T(8,128)(2,1)S(1)}, bf16[26,64,128]{2,1,0:T(8,128)(2,1)S(1)}, u32[]{:S(2)}, u32[]{:S(2)}) collective-permute-start(bf16[26,64,128]{2,1,0:T(8,128)(2,1)S(1)} %get-tuple-element.20), channel_id=1, source_target_pairs={{0,48},{8,24},{16,0},{24,40},{32,16},{40,56},{48,32},{56,8},{1,49}... | collective-permute-start | bytes 1277960 | tf_op jit(solution)/shard_map/ppermute | solution.py:237
  56.6 14.0 %collective-permute-start.3 = (bf16[36,64,128]{2,1,0:T(8,128)(2,1)S(1)}, bf16[36,64,128]{2,1,0:T(8,128)(2,1)S(1)}, u32[]{:S(2)}, u32[]{:S(2)}) collective-permute-start(bf16[36,64,128]{2,1,0:T(8,128)(2,1)S(1)} %pad_maximum_fusion), channel_id=1, source_target_pairs={{0,16},{8,56},{16,32},{24,8},{32,48},{40,24},{48,0},{56,40},{1,17}... | collective-permute-start | bytes 1769480 | tf_op jit(solution)/shard_map/ppermute | solution.py:237
  63.5 7.1 %collective-permute-start.5 = (bf16[21,64,128]{2,1,0:T(8,128)(2,1)S(1)}, bf16[21,64,128]{2,1,0:T(8,128)(2,1)S(1)}, u32[]{:S(2)}, u32[]{:S(2)}) collective-permute-start(bf16[21,64,128]{2,1,0:T(8,128)(2,1)S(1)} %slice.10), channel_id=1, source_target_pairs={{0,8},{8,0},{1,9},{9,1},{2,10},{10,2},{3,11},{11,3},{4,12},{12,4},... | collective-permute-start | bytes 1032200 | tf_op jit(solution)/shard_map/ppermute | solution.py:241
  67.1 8.5 %copy-start.1 = (s32[4,10]{1,0:T(4,128)S(1)}, s32[4,10]{1,0:T(4,128)}, u32[]{:S(2)}) copy-start(s32[4,10]{1,0:T(4,128)} %ancestors_hbm.1) | copy-start | bytes 484
  67.2 8.5 %copy-start.2 = (s32[4]{0:T(128)S(1)}, s32[4]{0:T(128)}, u32[]{:S(2)}) copy-start(s32[4]{0:T(128)} %depth_hbm.1) | copy-start | bytes 52
  67.2 3.4 %collective-permute-start.4 = (bf16[16,64,128]{2,1,0:T(8,128)(2,1)S(1)}, bf16[16,64,128]{2,1,0:T(8,128)(2,1)S(1)}, u32[]{:S(2)}, u32[]{:S(2)}) collective-permute-start(bf16[16,64,128]{2,1,0:T(8,128)(2,1)S(1)} %slice.9), channel_id=1, source_target_pairs={{0,8},{8,0},{1,9},{9,1},{2,10},{10,2},{3,11},{11,3},{4,12},{12,4},... | collective-permute-start | bytes 786440 | tf_op jit(solution)/shard_map/ppermute | solution.py:241
  70.6 5.0 %collective-permute-start.6 = (bf16[26,64,128]{2,1,0:T(8,128)(2,1)S(1)}, bf16[26,64,128]{2,1,0:T(8,128)(2,1)S(1)}, u32[]{:S(2)}, u32[]{:S(2)}) collective-permute-start(bf16[26,64,128]{2,1,0:T(8,128)(2,1)S(1)} %slice.11), channel_id=1, source_target_pairs={{0,8},{8,0},{1,9},{9,1},{2,10},{10,2},{3,11},{11,3},{4,12},{12,4},... | collective-permute-start | bytes 1277960 | tf_op jit(solution)/shard_map/ppermute | solution.py:241

commit v6 on v5

--- a/solution.py
+++ b/solution.py
@@ -124,15 +124,15 @@
 def early_kernel(pickers, own, near, far, mate, pairs):
     slabs = ((own, 0), (near, 10), (far, 0), (mate, 0))
 
-    def place_chip(chip, carry):
-        for core in range(2):
-            j = chip * 2 + core
+    def place_half(half, carry):
+        for shard in range(4):
+            j = half * 4 + shard
             pick = jnp.concatenate([pickers[j * 4 + n, :, :256] for n in range(4)], 0)
             got = jnp.dot(pick, gathered(slabs, 2, 2 * j), preferred_element_type=jnp.float32)
             pairs[j] = got.astype(jnp.bfloat16)
         return carry
 
-    lax.fori_loop(0, lax.axis_index("x") + 1, place_chip, 0)
+    lax.fori_loop(0, (lax.axis_index("x") + 2) >> 1, place_half, 0)
 
 
 def attend_kernel(
@@ -149,9 +149,9 @@
     slabs = ((across, 10), (first, 0), (second, 0), (rest, 5))
     parts = ((keep, 0), (across, 31), (far, 21), (mate, 16), (across, 0), (rest, 21), (second, 16), (rest, 0))
 
-    def place_chip(chip, carry):
-        for core in range(2):
-            j = chip * 2 + core
+    def place_half(half, carry):
+        for shard in range(4):
+            j = half * 4 + shard
             pick = jnp.concatenate([pickers[j * 4 + n, :, 256:] for n in range(4)], 0)
             got = jnp.dot(pick, gathered(slabs, 2, 2 * j), preferred_element_type=jnp.float32)
             got = (got + pairs[j].astype(jnp.float32)).astype(jnp.bfloat16)
@@ -160,7 +160,7 @@
                 values[j * 4 + n, :, :128] = got[n * 128 : (n + 1) * 128, 128:]
         return carry
 
-    lax.fori_loop(0, lax.axis_index("x") + 1, place_chip, 0)
+    lax.fori_loop(0, (lax.axis_index("x") + 2) >> 1, place_half, 0)
     raw = gathered(parts, GROUP)
     for n in range(4):
         got = jnp.dot(pickers[in_tree * 4 + n], raw, preferred_element_type=jnp.float32).astype(jnp.bfloat16)

time: 81.6 us -> 81.9 us (level)
  no operation moved by 1% of the time
where the time goes in v6:
time: 81.9 us; the launch traced here: 81.3 us
  blocking collectives  42.1 us (51%)
  starting transfers between devices  23.9 us (29%)
  Pallas kernels  9.27 us (11%)
  waiting for transfers between devices  5.51 us (7%)
    all_to_all x1, blocking collectives, exchange(): return lax.all_to_all(block, axes, split_axis=0, concat_axis=0, tiled=True)  42.1 us
    ppermute x4, starting transfers between devices, swap(): return lax.ppermute(block, 'c', [(0, 1), (1, 0)])  13 us
    ppermute x3, starting transfers between devices, ring(): return lax.ppermute(block, ('x', 'c'), route)  10.9 us
    pallas_call x1, Pallas kernels, finish(): pl.pallas_call(attend_kernel, out_shape=jax.ShapeDtypeStruct((512, 640),...  5.48 us
    ppermute x3, waiting for transfers between devices, ring(): return lax.ppermute(block, ('x', 'c'), route)  3.09 us
    pallas_call x1, Pallas kernels, body(): pl.pallas_call(sort_kernel, out_shape=jax.ShapeDtypeStruct((8, 8, 8, 896)...  2.48 us
    ppermute x4, waiting for transfers between devices, swap(): return lax.ppermute(block, 'c', [(0, 1), (1, 0)])  2.42 us
  transfers between devices with their start and end apart: 7, of which 3 were waited for; matrix products, arithmetic and copies ran while one was open for 0% of the time, Pallas kernels for 1%

profile of v6, /device:TPU:1, one launch (start us, length us, event | category | flops | bytes accessed | tf_op | source)
XLA Modules:
  0.0 81.3 jit_solution(12562431529897079303)
XLA Ops:
  0.0 0.0 copy-start
  0.0 2.5 %sort_rows.1 = bf16[8,8,8,896]{3,2,1,0:T(8,128)(2,1)} custom-call(s32[256,128]{1,0:T(8,128)} %bitcast.2, bf16[64,5120]{1,0:T(8,128)(2,1)} %query_hbm.1, bf16[64,2048]{1,0:T(8,128)(2,1)} %pairs_hbm.1), custom_call_target="tpu_custom_call" | custom-call | tf_op jit(solution)/shard_map/sort_rows/pallas_call | solution.py:298
  2.5 42.1 %all_to_all.5.landed = bf16[64,8,896]{2,1,0:T(8,128)(2,1)S(1)} all-to-all(bf16[64,8,896]{2,1,0:T(8,128)(2,1)} %bitcast.4), channel_id=1, replica_groups=mesh['z'=8,'x'=4,'c'=2,'t'=8] {'z','t'}, dimensions={0} | all-to-all | bytes 1835008 | tf_op jit(solution)/shard_map/all_to_all | solution.py:245
  44.6 0.5 regroup.1
  45.1 4.4 %collective-permute-start.1 = (bf16[26,64,128]{2,1,0:T(8,128)(2,1)S(1)}, bf16[26,64,128]{2,1,0:T(8,128)(2,1)S(1)}, u32[]{:S(2)}, u32[]{:S(2)}) collective-permute-start(bf16[26,64,128]{2,1,0:T(8,128)(2,1)S(1)} %get-tuple-element.24), channel_id=1, source_target_pairs={{0,16},{8,56},{16,32},{24,8},{32,48},{40,24},{48,0},{56,40},{1,17}... | collective-permute-start | bytes 1277960 | tf_op jit(solution)/shard_map/ppermute | solution.py:237
  49.5 3.9 %collective-permute-start.2 = (bf16[21,64,128]{2,1,0:T(8,128)(2,1)S(1)}, bf16[21,64,128]{2,1,0:T(8,128)(2,1)S(1)}, u32[]{:S(2)}, u32[]{:S(2)}) collective-permute-start(bf16[21,64,128]{2,1,0:T(8,128)(2,1)S(1)} %get-tuple-element.25.own), channel_id=1, source_target_pairs={{0,8},{8,0},{1,9},{9,1},{2,10},{10,2},{3,11},{11,3},{4,12},{12,4},... | collective-permute-start | bytes 1032200 | tf_op jit(solution)/shard_map/ppermute | solution.py:241
  53.4 3.1 %collective-permute-start = (bf16[26,64,128]{2,1,0:T(8,128)(2,1)S(1)}, bf16[26,64,128]{2,1,0:T(8,128)(2,1)S(1)}, u32[]{:S(2)}, u32[]{:S(2)}) collective-permute-start(bf16[26,64,128]{2,1,0:T(8,128)(2,1)S(1)} %get-tuple-element.20), channel_id=1, source_target_pairs={{0,48},{8,24},{16,0},{24,40},{32,16},{40,56},{48,32},{56,8},{1,49}... | collective-permute-start | bytes 1277960 | tf_op jit(solution)/shard_map/ppermute | solution.py:237
  56.5 0.0 collective-permute-done.2.mate
  56.5 0.0 collective-permute-done.1.near
  56.5 0.1 pad_maximum_fusion
  56.6 3.4 %collective-permute-start.3 = (bf16[36,64,128]{2,1,0:T(8,128)(2,1)S(1)}, bf16[36,64,128]{2,1,0:T(8,128)(2,1)S(1)}, u32[]{:S(2)}, u32[]{:S(2)}) collective-permute-start(bf16[36,64,128]{2,1,0:T(8,128)(2,1)S(1)} %pad_maximum_fusion), channel_id=1, source_target_pairs={{0,16},{8,56},{16,32},{24,8},{32,48},{40,24},{48,0},{56,40},{1,17}... | collective-permute-start | bytes 1769480 | tf_op jit(solution)/shard_map/ppermute | solution.py:237
  60.0 0.0 copy-done
  60.0 0.4 pickers.1
  60.4 3.1 %collective-permute-done.far = bf16[26,64,128]{2,1,0:T(8,128)(2,1)S(1)} collective-permute-done((bf16[26,64,128]{2,1,0:T(8,128)(2,1)S(1)}, bf16[26,64,128]{2,1,0:T(8,128)(2,1)S(1)}, u32[]{:S(2)}, u32[]{:S(2)}) %collective-permute-start) | collective-permute-done | bytes 426016 | tf_op jit(solution)/shard_map/ppermute | solution.py:237
  63.5 3.6 %collective-permute-start.5 = (bf16[21,64,128]{2,1,0:T(8,128)(2,1)S(1)}, bf16[21,64,128]{2,1,0:T(8,128)(2,1)S(1)}, u32[]{:S(2)}, u32[]{:S(2)}) collective-permute-start(bf16[21,64,128]{2,1,0:T(8,128)(2,1)S(1)} %slice.10), channel_id=1, source_target_pairs={{0,8},{8,0},{1,9},{9,1},{2,10},{10,2},{3,11},{11,3},{4,12},{12,4},... | collective-permute-start | bytes 1032200 | tf_op jit(solution)/shard_map/ppermute | solution.py:241
  67.1 0.0 copy-start.1
  67.2 0.0 copy-start.2
  67.2 1.9 %collective-permute-start.4 = (bf16[16,64,128]{2,1,0:T(8,128)(2,1)S(1)}, bf16[16,64,128]{2,1,0:T(8,128)(2,1)S(1)}, u32[]{:S(2)}, u32[]{:S(2)}) collective-permute-start(bf16[16,64,128]{2,1,0:T(8,128)(2,1)S(1)} %slice.9), channel_id=1, source_target_pairs={{0,8},{8,0},{1,9},{9,1},{2,10},{10,2},{3,11},{11,3},{4,12},{12,4},... | collective-permute-start | bytes 786440 | tf_op jit(solution)/shard_map/ppermute | solution.py:241
  69.1 0.5 place_early.1.pairs
  69.6 1.0 %collective-permute-done.4.first = bf16[16,64,128]{2,1,0:T(8,128)(2,1)S(1)} collective-permute-done((bf16[16,64,128]{2,1,0:T(8,128)(2,1)S(1)}, bf16[16,64,128]{2,1,0:T(8,128)(2,1)S(1)}, u32[]{:S(2)}, u32[]{:S(2)}) %collective-permute-start.4) | collective-permute-done | bytes 262176 | tf_op jit(solution)/shard_map/ppermute | solution.py:241
  70.6 0.0 collective-permute-done.5.second
  70.6 0.0 collective-permute-done.3.across
  70.6 3.6 %collective-permute-start.6 = (bf16[26,64,128]{2,1,0:T(8,128)(2,1)S(1)}, bf16[26,64,128]{2,1,0:T(8,128)(2,1)S(1)}, u32[]{:S(2)}, u32[]{:S(2)}) collective-permute-start(bf16[26,64,128]{2,1,0:T(8,128)(2,1)S(1)} %slice.11), channel_id=1, source_target_pairs={{0,8},{8,0},{1,9},{9,1},{2,10},{10,2},{3,11},{11,3},{4,12},{12,4},... | collective-permute-start | bytes 1277960 | tf_op jit(solution)/shard_map/ppermute | solution.py:241
  74.3 1.4 %collective-permute-done.6.rest = bf16[26,64,128]{2,1,0:T(8,128)(2,1)S(1)} collective-permute-done((bf16[26,64,128]{2,1,0:T(8,128)(2,1)S(1)}, bf16[26,64,128]{2,1,0:T(8,128)(2,1)S(1)}, u32[]{:S(2)}, u32[]{:S(2)}) %collective-permute-start.6) | collective-permute-done | bytes 426016 | tf_op jit(solution)/shard_map/ppermute | solution.py:241
  75.6 0.0 copy-done.1
  75.7 0.0 copy-done.2
  75.7 5.5 %tree_attention.1 = bf16[512,640]{1,0:T(8,128)(2,1)} custom-call(s32[4,10]{1,0:T(4,128)S(1)} %copy-done.1, s32[4]{0:T(128)S(1)} %copy-done.2, bf16[32,128,512]{2,1,0:T(8,128)(2,1)S(1)} %pickers.1, bf16[8,512,256]{2,1,0:T(8,128)(2,1)S(1)} %place_early.1.pairs, bf16[5,64,128]{2,1,0:T(8,128)(2,1)S(1)} %get-tuple-element.31.keep, ...), custom_call_target="tpu_custom_call" | custom-call | tf_op jit(solution)/shard_map/tree_attention/pallas_call | solution.py:271
  (3 shorter events, 0.1 us)
Async XLA Ops:
  0.0 60.0 %copy-start = (s32[32768]{0:T(1024)S(1)}, s32[32768]{0:T(1024)}, u32[]{:S(2)}) copy-start(s32[32768]{0:T(1024)} %param.7) | copy-start | bytes 393220
  45.1 11.4 %collective-permute-start.1 = (bf16[26,64,128]{2,1,0:T(8,128)(2,1)S(1)}, bf16[26,64,128]{2,1,0:T(8,128)(2,1)S(1)}, u32[]{:S(2)}, u32[]{:S(2)}) collective-permute-start(bf16[26,64,128]{2,1,0:T(8,128)(2,1)S(1)} %get-tuple-element.24), channel_id=1, source_target_pairs={{0,16},{8,56},{16,32},{24,8},{32,48},{40,24},{48,0},{56,40},{1,17}... | collective-permute-start | bytes 1277960 | tf_op jit(solution)/shard_map/ppermute | solution.py:237
  49.5 7.0 %collective-permute-start.2 = (bf16[21,64,128]{2,1,0:T(8,128)(2,1)S(1)}, bf16[21,64,128]{2,1,0:T(8,128)(2,1)S(1)}, u32[]{:S(2)}, u32[]{:S(2)}) collective-permute-start(bf16[21,64,128]{2,1,0:T(8,128)(2,1)S(1)} %get-tuple-element.25.own), channel_id=1, source_target_pairs={{0,8},{8,0},{1,9},{9,1},{2,10},{10,2},{3,11},{11,3},{4,12},{12,4},... | collective-permute-start | bytes 1032200 | tf_op jit(solution)/shard_map/ppermute | solution.py:241
  53.4 10.1 %collective-permute-start = (bf16[26,64,128]{2,1,0:T(8,128)(2,1)S(1)}, bf16[26,64,128]{2,1,0:T(8,128)(2,1)S(1)}, u32[]{:S(2)}, u32[]{:S(2)}) collective-permute-start(bf16[26,64,128]{2,1,0:T(8,128)(2,1)S(1)} %get-tuple-element.20), channel_id=1, source_target_pairs={{0,48},{8,24},{16,0},{24,40},{32,16},{40,56},{48,32},{56,8},{1,49}... | collective-permute-start | bytes 1277960 | tf_op jit(solution)/shard_map/ppermute | solution.py:237
  56.6 14.0 %collective-permute-start.3 = (bf16[36,64,128]{2,1,0:T(8,128)(2,1)S(1)}, bf16[36,64,128]{2,1,0:T(8,128)(2,1)S(1)}, u32[]{:S(2)}, u32[]{:S(2)}) collective-permute-start(bf16[36,64,128]{2,1,0:T(8,128)(2,1)S(1)} %pad_maximum_fusion), channel_id=1, source_target_pairs={{0,16},{8,56},{16,32},{24,8},{32,48},{40,24},{48,0},{56,40},{1,17}... | collective-permute-start | bytes 1769480 | tf_op jit(solution)/shard_map/ppermute | solution.py:237
  63.5 7.1 %collective-permute-start.5 = (bf16[21,64,128]{2,1,0:T(8,128)(2,1)S(1)}, bf16[21,64,128]{2,1,0:T(8,128)(2,1)S(1)}, u32[]{:S(2)}, u32[]{:S(2)}) collective-permute-start(bf16[21,64,128]{2,1,0:T(8,128)(2,1)S(1)} %slice.10), channel_id=1, source_target_pairs={{0,8},{8,0},{1,9},{9,1},{2,10},{10,2},{3,11},{11,3},{4,12},{12,4},... | collective-permute-start | bytes 1032200 | tf_op jit(solution)/shard_map/ppermute | solution.py:241
  67.1 8.5 %copy-start.1 = (s32[4,10]{1,0:T(4,128)S(1)}, s32[4,10]{1,0:T(4,128)}, u32[]{:S(2)}) copy-start(s32[4,10]{1,0:T(4,128)} %ancestors_hbm.1) | copy-start | bytes 484
  67.2 8.5 %copy-start.2 = (s32[4]{0:T(128)S(1)}, s32[4]{0:T(128)}, u32[]{:S(2)}) copy-start(s32[4]{0:T(128)} %depth_hbm.1) | copy-start | bytes 52
  67.2 3.4 %collective-permute-start.4 = (bf16[16,64,128]{2,1,0:T(8,128)(2,1)S(1)}, bf16[16,64,128]{2,1,0:T(8,128)(2,1)S(1)}, u32[]{:S(2)}, u32[]{:S(2)}) collective-permute-start(bf16[16,64,128]{2,1,0:T(8,128)(2,1)S(1)} %slice.9), channel_id=1, source_target_pairs={{0,8},{8,0},{1,9},{9,1},{2,10},{10,2},{3,11},{11,3},{4,12},{12,4},... | collective-permute-start | bytes 786440 | tf_op jit(solution)/shard_map/ppermute | solution.py:241
  70.6 5.0 %collective-permute-start.6 = (bf16[26,64,128]{2,1,0:T(8,128)(2,1)S(1)}, bf16[26,64,128]{2,1,0:T(8,128)(2,1)S(1)}, u32[]{:S(2)}, u32[]{:S(2)}) collective-permute-start(bf16[26,64,128]{2,1,0:T(8,128)(2,1)S(1)} %slice.11), channel_id=1, source_target_pairs={{0,8},{8,0},{1,9},{9,1},{2,10},{10,2},{3,11},{11,3},{4,12},{12,4},... | collective-permute-start | bytes 1277960 | tf_op jit(solution)/shard_map/ppermute | solution.py:241
